TPU v7x, 32 devices: a whole 2x2x4 slice. The times are simulated.
32 devices in a mesh: segment: 4 (over x, core), expert: 4 (over z), fsdp: 2 (over y).
Axes of the slice: x: 2, y: 2, z: 4, core: 2. Of those that a mesh axis runs over, the one named last changes fastest.
Arguments:
- acts: bfloat16 [4, 2, 128, 1024], P('segment', None, ('expert', 'fsdp')), may hold values from -6 to 6
- out_grad: bfloat16 [2, 128, 1024], P(None, ('expert', 'fsdp')), may hold values from -6 to 6
- expert_ids: int32 [4, 2, 128, 2], P('segment', None, ('expert', 'fsdp')), may hold values from 0 to 3, all different within a row; in each aligned block of 16 rows (0 to 15, 16 to 31, ..., all dimensions but the last counted through in order) at most 10 rows name the same one
- gates: bfloat16 [4, 2, 128, 2], P('segment', None, ('expert', 'fsdp')), may hold values from 0.19921875 to 1
- w_gate: bfloat16 [4, 4, 1024, 2048], P('segment', 'expert', None, 'fsdp'), may hold values from -0.1875 to 0.1875
- w_up: bfloat16 [4, 4, 1024, 2048], P('segment', 'expert', None, 'fsdp'), may hold values from -0.1875 to 0.1875
- w_down: bfloat16 [4, 4, 2048, 1024], P('segment', 'expert', 'fsdp'), may hold values from -0.125 to 0.125
Outputs:
- act_grad: bfloat16 [4, 2, 128, 1024], P('segment', None, ('expert', 'fsdp'))
- gate_grad: float32 [4, 2, 128, 2], P('segment', None, ('expert', 'fsdp'))
- grad_w_gate: bfloat16 [4, 4, 1024, 2048], P('segment', 'expert', None, 'fsdp')
- grad_w_up: bfloat16 [4, 4, 1024, 2048], P('segment', 'expert', None, 'fsdp')
- grad_w_down: bfloat16 [4, 4, 2048, 1024], P('segment', 'expert', 'fsdp')
Inputs may be any that keep to these rules, and one draw needn't show every extreme that they name: `expert_ids`: each row names 2 different experts. Within the tokens of one device for one layer and micro-batch (aligned blocks of 16 rows) no expert is named by more than 10 tokens, and in some such block an expert is named by exactly 10.
All inputs are finite; a program needn't handle non-finite values.
Results may differ from a plain program's by a relative error of at most 0.035.
Values may be sent and summed in bfloat16 or wider, within the bound.
A program may use at most 64 MiB of HBM per device.

v0:
```python
import jax
import jax.numpy as jnp
from jax import lax
from jax.sharding import PartitionSpec as P


def from_behind(value, axis, steps):
    count = lax.axis_size(axis)
    leading, last = (max(0, -steps), min(count, count - steps))
    return lax.ppermute(value, axis, [(source, source + steps) for source in range(leading, last)])


def silu_parts(pre_gate):
    sigmoid = jax.nn.sigmoid(pre_gate)
    return (pre_gate * sigmoid, sigmoid * (1.0 + pre_gate * (1.0 - sigmoid)))


def local(acts, out_grad, expert_ids, gates, w_gate, w_up, w_down):
    segments = lax.axis_size("segment")
    segment_now = lax.axis_index("segment")
    n_expert = lax.axis_size("expert")
    n_fsdp = lax.axis_size("fsdp")
    micro_count = acts.shape[1]
    tok_count = acts.shape[2]
    width = acts.shape[3]
    top_count = expert_ids.shape[3]
    capacity = 5 * top_count * tok_count // (4 * n_expert)
    w_first = w_gate[0, 0]
    w_third = w_up[0, 0]
    w_second = w_down[0, 0]
    hid_local = w_first.shape[1]
    expert_iota = jnp.arange(n_expert, dtype=jnp.int32)
    slot_iota = jnp.arange(capacity, dtype=jnp.int32)
    micro_iota = jnp.arange(micro_count, dtype=jnp.int32)
    contract_rows = (((0,), (0,)), ((), ()))
    contract_cols = (((1,), (1,)), ((), ()))
    grad_first = jnp.zeros((width, hid_local), jnp.float32)
    grad_third = jnp.zeros((width, hid_local), jnp.float32)
    grad_second = jnp.zeros((hid_local, width), jnp.float32)
    act_out = jnp.zeros(acts.shape, jnp.bfloat16)
    gate_out = jnp.zeros(gates.shape, jnp.float32)
    previous = jnp.zeros((tok_count, width), jnp.bfloat16)
    for moment in range(micro_count + segments - 1):
        micro_index = moment - (segments - 1 - segment_now)
        valid = (micro_index >= 0) & (micro_index < micro_count)
        picked = jnp.clip(micro_index, 0, micro_count - 1)
        tokens_now = lax.dynamic_index_in_dim(acts[0], picked, 0, keepdims=False)
        loss_grad = lax.dynamic_index_in_dim(out_grad, picked, 0, keepdims=False)
        ids_now = lax.dynamic_index_in_dim(expert_ids[0], picked, 0, keepdims=False)
        gates_now = lax.dynamic_index_in_dim(gates[0], picked, 0, keepdims=False)
        if moment > 0:
            incoming = from_behind(previous, "segment", -1)
        else:
            incoming = previous
        grad_now = jnp.where(segment_now == segments - 1, loss_grad, incoming)
        table = (ids_now[:, :, None] == expert_iota).astype(jnp.int32)
        counts = jnp.sum(table, axis=1)
        before = jnp.cumsum(counts, axis=0) - counts
        slots = jnp.sum(before[:, None, :] * table, axis=2)
        routing = (
            (ids_now[None, None] == expert_iota[:, None, None, None])
            & (slots[None, None] == slot_iota[None, :, None, None])
        ).astype(jnp.float32)
        placing = jnp.sum(routing, axis=3).astype(jnp.bfloat16)
        token_buf = jnp.einsum(
            "ect,td->ecd", placing, tokens_now, preferred_element_type=jnp.float32
        ).astype(jnp.bfloat16)
        grad_buf = jnp.einsum(
            "ect,td->ecd", placing, grad_now, preferred_element_type=jnp.float32
        ).astype(jnp.bfloat16)
        gate_buf = jnp.einsum("ectk,tk->ec", routing, gates_now.astype(jnp.float32)).astype(
            jnp.bfloat16
        )
        start_state = (
            grad_first,
            grad_third,
            grad_second,
            jnp.zeros((n_fsdp, n_expert, capacity, width), jnp.bfloat16),
            jnp.zeros((n_fsdp, n_expert, capacity), jnp.bfloat16),
        )
        grouped = (
            lax.all_gather(token_buf[None], "fsdp", axis=0, tiled=True),
            lax.all_gather(grad_buf[None], "fsdp", axis=0, tiled=True),
            lax.all_gather(gate_buf[None], "fsdp", axis=0, tiled=True),
        )
        token_rows = lax.all_to_all(grouped[0], "expert", split_axis=1, concat_axis=1, tiled=True)
        grad_rows = lax.all_to_all(grouped[1], "expert", split_axis=1, concat_axis=1, tiled=True)
        gate_rows = lax.all_to_all(grouped[2], "expert", split_axis=1, concat_axis=1, tiled=True)

        def compute(state):
            sum_first, sum_third, sum_second, part_rows, part_gates = state
            flat_tokens = token_rows.reshape(-1, width)
            flat_grads = grad_rows.reshape(-1, width)
            gate_col = gate_rows.reshape(-1).astype(jnp.float32)[:, None]
            pre_gate = jnp.dot(flat_tokens, w_first, preferred_element_type=jnp.float32)
            pre_up = jnp.dot(flat_tokens, w_third, preferred_element_type=jnp.float32)
            activated, slope_term = silu_parts(pre_gate)
            hidden = activated * pre_up
            back_hidden = lax.dot_general(
                flat_grads, w_second, contract_cols, preferred_element_type=jnp.float32
            )
            scaled = back_hidden * gate_col
            grad_gate_pre = (scaled * pre_up * slope_term).astype(jnp.bfloat16)
            grad_up_pre = (scaled * activated).astype(jnp.bfloat16)
            hidden_gated = (hidden * gate_col).astype(jnp.bfloat16)
            sum_first = sum_first + lax.dot_general(
                flat_tokens, grad_gate_pre, contract_rows, preferred_element_type=jnp.float32
            )
            sum_third = sum_third + lax.dot_general(
                flat_tokens, grad_up_pre, contract_rows, preferred_element_type=jnp.float32
            )
            sum_second = sum_second + lax.dot_general(
                hidden_gated, flat_grads, contract_rows, preferred_element_type=jnp.float32
            )
            partial_value = lax.dot_general(
                grad_gate_pre, w_first, contract_cols, preferred_element_type=jnp.float32
            )
            partial_value = partial_value + lax.dot_general(
                grad_up_pre, w_third, contract_cols, preferred_element_type=jnp.float32
            )
            gate_part = jnp.sum(hidden * back_hidden, axis=1)
            part_rows = partial_value.astype(jnp.bfloat16).reshape(token_rows.shape)
            part_gates = gate_part.astype(jnp.bfloat16).reshape(gate_rows.shape)
            return (sum_first, sum_third, sum_second, part_rows, part_gates)

        finished = lax.cond(valid, compute, lambda state: state, start_state)
        grad_first, grad_third, grad_second, part_rows, part_gates = finished
        summed_rows, summed_gates = (
            lax.psum_scatter(part_rows, "fsdp", scatter_dimension=0, tiled=True).astype(
                jnp.float32
            ),
            lax.psum_scatter(part_gates, "fsdp", scatter_dimension=0, tiled=True).astype(
                jnp.float32
            ),
        )
        back_rows, back_gates = (
            lax.all_to_all(
                summed_rows[0].astype(jnp.bfloat16),
                "expert",
                split_axis=0,
                concat_axis=0,
                tiled=True,
            ),
            lax.all_to_all(
                summed_gates[0].astype(jnp.bfloat16),
                "expert",
                split_axis=0,
                concat_axis=0,
                tiled=True,
            ),
        )
        token_back = jnp.einsum(
            "ect,ecd->td", placing, back_rows, preferred_element_type=jnp.float32
        )
        new_grad = (grad_now.astype(jnp.float32) + token_back).astype(jnp.bfloat16)
        gate_new = jnp.einsum("ectk,ec->tk", routing, back_gates.astype(jnp.float32))
        chosen = micro_iota == micro_index
        act_out = jnp.where(chosen[None, :, None, None], new_grad[None, None], act_out)
        gate_out = jnp.where(chosen[None, :, None, None], gate_new[None, None], gate_out)
        previous = new_grad
    return (
        act_out,
        gate_out,
        grad_first.astype(jnp.bfloat16)[None, None],
        grad_third.astype(jnp.bfloat16)[None, None],
        grad_second.astype(jnp.bfloat16)[None, None],
    )


def solution(mesh):
    in_specs = (
        P("segment", None, ("expert", "fsdp"), None),
        P(None, ("expert", "fsdp"), None),
        P("segment", None, ("expert", "fsdp"), None),
        P("segment", None, ("expert", "fsdp"), None),
        P("segment", "expert", None, "fsdp"),
        P("segment", "expert", None, "fsdp"),
        P("segment", "expert", "fsdp", None),
    )
    out_specs = (
        P("segment", None, ("expert", "fsdp"), None),
        P("segment", None, ("expert", "fsdp"), None),
        P("segment", "expert", None, "fsdp"),
        P("segment", "expert", None, "fsdp"),
        P("segment", "expert", "fsdp", None),
    )
    return jax.shard_map(local, mesh=mesh, in_specs=in_specs, out_specs=out_specs, check_vma=False)
```

profile of v0, /device:TPU:0, one launch (start us, length us, event | category | flops | bytes accessed | tf_op | source)
XLA Modules:
  0.0 476.6 jit_solution(16303511642988975964)
XLA Ops:
  10.0 5.2 %all-gather.15 = bf16[2,4,10]{2,1,0:T(4,128)(2,1)S(1)} all-gather(bf16[1,4,10]{2,1,0:T(4,128)(2,1)S(1)} %convert_bitcast_fusion.7), channel_id=3, replica_groups=mesh['segment'=4,'expert'=4,'fsdp'=2] {'fsdp'}, dimensions={0}, use_global_device_ids=true | all-gather | bytes 240 | tf_op jit(solution)/shard_map/all_gather | solution.py:84
  15.7 5.4 %all-to-all-start.1 = ((bf16[2,4,10]{2,0,1:T(2,128)(2,1)}), bf16[2,4,10]{2,0,1:T(2,128)(2,1)S(1)}, u32[]{:S(2)}, u32[]{:S(2)}) async-start(bf16[2,4,10]{2,0,1:T(2,128)(2,1)} %copy.180), calls=%async_computation.1 | async-start | bytes 4096 | tf_op jit(solution)/shard_map/all_to_all | solution.py:88
  23.2 5.6 %all-gather = bf16[8,10,1024]{2,1,0:T(8,128)(2,1)S(1)} all-gather(bf16[4,10,1024]{2,1,0:T(8,128)(2,1)S(1)} %convolution_convert_fusion.9), channel_id=2, replica_groups=mesh['segment'=4,'expert'=4,'fsdp'=2] {'fsdp'}, dimensions={0}, use_global_device_ids=true | all-gather | bytes 245760 | tf_op jit(solution)/shard_map/all_gather | solution.py:83
  29.7 5.1 %all-to-all-start = ((bf16[2,4,10,1024]{3,0,2,1:T(2,128)(2,1)}), bf16[2,4,10,1024]{3,0,2,1:T(2,128)(2,1)S(1)}, u32[]{:S(2)}, u32[]{:S(2)}) async-start(bf16[2,4,10,1024]{3,0,2,1:T(2,128)(2,1)} %copy.179), calls=%async_computation | async-start | bytes 327680 | tf_op jit(solution)/shard_map/all_to_all | solution.py:87
  34.8 5.6 %all-gather.2 = bf16[8,10,1024]{2,1,0:T(8,128)(2,1)S(1)} all-gather(bf16[4,10,1024]{2,1,0:T(8,128)(2,1)S(1)} %convolution_convert_fusion.8), channel_id=4, replica_groups=mesh['segment'=4,'expert'=4,'fsdp'=2] {'fsdp'}, dimensions={0}, use_global_device_ids=true | all-gather | bytes 245760 | tf_op jit(solution)/shard_map/all_gather | solution.py:82
  41.4 5.1 %all-to-all-start.2 = ((bf16[2,4,10,1024]{3,0,2,1:T(2,128)(2,1)}), bf16[2,4,10,1024]{3,0,2,1:T(2,128)(2,1)S(1)}, u32[]{:S(2)}, u32[]{:S(2)}) async-start(bf16[2,4,10,1024]{3,0,2,1:T(2,128)(2,1)} %copy.182), calls=%async_computation.2 | async-start | bytes 327680 | tf_op jit(solution)/shard_map/all_to_all | solution.py:86
  52.6 7.7 %conditional.5 = (f32[1024,1024]{0,1:T(8,128)}, f32[1024,1024]{0,1:T(8,128)}, f32[1024,1024]{1,0:T(8,128)}, bf16[2,4,10,1024]{3,2,1,0:T(8,128)(2,1)S(1)}, bf16[2,4,10]{2,1,0:T(4,128)(2,1)S(1)}) conditional(s32[]{:T(128)} %convert_element_type.388, () %tuple.48, (bf16[2,4,10,1024]{3,0,2,1:T(2,128)(2,1)S(1)}, bf16[1024,1024]{1,0:T(8,128)(2,1)}, ...), branch_computations={%region_4.5_spmd, %region_5.7_spmd} | conditional | flops 1344307200 | bytes 46893372 | solution.py:126
  61.4 16.1 %reduce-scatter.6.cloned.1.call-done = bf16[1,4,10,1024]{3,2,1,0:T(8,128)(2,1)} async-done(((bf16[2,4,10,1024]{3,2,1,0:T(8,128)(2,1)}), bf16[1,4,10,1024]{3,2,1,0:T(8,128)(2,1)}) %reduce-scatter.6.cloned.1.call-update) | async-done | bytes 81936 | tf_op jit(solution)/shard_map/reduce_scatter | solution.py:129
  93.6 6.9 %all-gather.5 = bf16[8,10,1024]{2,1,0:T(8,128)(2,1)S(1)} all-gather(bf16[4,10,1024]{2,1,0:T(8,128)(2,1)S(1)} %convolution_convert_fusion.6), channel_id=7, replica_groups=mesh['segment'=4,'expert'=4,'fsdp'=2] {'fsdp'}, dimensions={0}, use_global_device_ids=true | all-gather | bytes 245760 | tf_op jit(solution)/shard_map/all_gather | solution.py:82
  101.8 5.1 %all-to-all-start.6 = ((bf16[2,4,10,1024]{3,0,2,1:T(2,128)(2,1)}), bf16[2,4,10,1024]{3,0,2,1:T(2,128)(2,1)S(1)}, u32[]{:S(2)}, u32[]{:S(2)}) async-start(bf16[2,4,10,1024]{3,0,2,1:T(2,128)(2,1)} %copy.194), calls=%async_computation.7 | async-start | bytes 327680 | tf_op jit(solution)/shard_map/all_to_all | solution.py:86
  107.1 5.9 %all-gather.3 = bf16[8,10,1024]{2,1,0:T(8,128)(2,1)S(1)} all-gather(bf16[4,10,1024]{2,1,0:T(8,128)(2,1)S(1)} %convolution_convert_fusion.7), channel_id=5, replica_groups=mesh['segment'=4,'expert'=4,'fsdp'=2] {'fsdp'}, dimensions={0}, use_global_device_ids=true | all-gather | bytes 245760 | tf_op jit(solution)/shard_map/all_gather | solution.py:83
  127.3 34.2 %reduce-scatter.8.cloned.1.call-done = bf16[1,4,10,1024]{3,2,1,0:T(8,128)(2,1)} async-done(((bf16[2,4,10,1024]{3,2,1,0:T(8,128)(2,1)}), bf16[1,4,10,1024]{3,2,1,0:T(8,128)(2,1)}) %reduce-scatter.8.cloned.1.call-update) | async-done | bytes 81936 | tf_op jit(solution)/shard_map/reduce_scatter | solution.py:129
  166.1 6.0 %all-to-all-done.7 = bf16[4,10,1024]{2,1,0:T(8,128)(2,1)S(1)} async-done(((bf16[4,10,1024]{2,1,0:T(8,128)(2,1)}), bf16[4,10,1024]{2,1,0:T(8,128)(2,1)S(1)}, u32[]{:S(2)}, u32[]{:S(2)}) %all-to-all-start.7) | async-done | bytes 81952 | tf_op jit(solution)/shard_map/all_to_all | solution.py:137
  176.9 6.9 %all-gather.8 = bf16[8,10,1024]{2,1,0:T(8,128)(2,1)S(1)} all-gather(bf16[4,10,1024]{2,1,0:T(8,128)(2,1)S(1)} %convolution_convert_fusion.4), channel_id=10, replica_groups=mesh['segment'=4,'expert'=4,'fsdp'=2] {'fsdp'}, dimensions={0}, use_global_device_ids=true | all-gather | bytes 245760 | tf_op jit(solution)/shard_map/all_gather | solution.py:82
  189.9 5.9 %all-gather.6 = bf16[8,10,1024]{2,1,0:T(8,128)(2,1)S(1)} all-gather(bf16[4,10,1024]{2,1,0:T(8,128)(2,1)S(1)} %convolution_convert_fusion.5), channel_id=8, replica_groups=mesh['segment'=4,'expert'=4,'fsdp'=2] {'fsdp'}, dimensions={0}, use_global_device_ids=true | all-gather | bytes 245760 | tf_op jit(solution)/shard_map/all_gather | solution.py:83
  209.9 32.8 %reduce-scatter.10.cloned.1.call-done = bf16[1,4,10,1024]{3,2,1,0:T(8,128)(2,1)} async-done(((bf16[2,4,10,1024]{3,2,1,0:T(8,128)(2,1)}), bf16[1,4,10,1024]{3,2,1,0:T(8,128)(2,1)}) %reduce-scatter.10.cloned.1.call-update) | async-done | bytes 81936 | tf_op jit(solution)/shard_map/reduce_scatter | solution.py:129
  248.0 5.4 %all-to-all-done.11 = bf16[4,10,1024]{2,1,0:T(8,128)(2,1)S(1)} async-done(((bf16[4,10,1024]{2,1,0:T(8,128)(2,1)}), bf16[4,10,1024]{2,1,0:T(8,128)(2,1)S(1)}, u32[]{:S(2)}, u32[]{:S(2)}) %all-to-all-start.11) | async-done | bytes 81952 | tf_op jit(solution)/shard_map/all_to_all | solution.py:137
  258.1 6.9 %all-gather.11 = bf16[8,10,1024]{2,1,0:T(8,128)(2,1)S(1)} all-gather(bf16[4,10,1024]{2,1,0:T(8,128)(2,1)S(1)} %convolution_convert_fusion.2), channel_id=13, replica_groups=mesh['segment'=4,'expert'=4,'fsdp'=2] {'fsdp'}, dimensions={0}, use_global_device_ids=true | all-gather | bytes 245760 | tf_op jit(solution)/shard_map/all_gather | solution.py:82
  271.1 6.1 %all-gather.9 = bf16[8,10,1024]{2,1,0:T(8,128)(2,1)S(1)} all-gather(bf16[4,10,1024]{2,1,0:T(8,128)(2,1)S(1)} %convolution_convert_fusion.3), channel_id=11, replica_groups=mesh['segment'=4,'expert'=4,'fsdp'=2] {'fsdp'}, dimensions={0}, use_global_device_ids=true | all-gather | bytes 245760 | tf_op jit(solution)/shard_map/all_gather | solution.py:83
  283.1 5.8 %all-to-all-done.12 = bf16[2,4,10,1024]{3,0,2,1:T(2,128)(2,1)S(1)} async-done(((bf16[2,4,10,1024]{3,0,2,1:T(2,128)(2,1)}), bf16[2,4,10,1024]{3,0,2,1:T(2,128)(2,1)S(1)}, u32[]{:S(2)}, u32[]{:S(2)}) %all-to-all-start.12) | async-done | bytes 163872 | tf_op jit(solution)/shard_map/all_to_all | solution.py:87
  288.9 22.7 %conditional.8 = (f32[1024,1024]{0,1:T(8,128)}, f32[1024,1024]{0,1:T(8,128)}, f32[1024,1024]{1,0:T(8,128)}, bf16[2,4,10,1024]{3,2,1,0:T(8,128)(2,1)S(1)}, bf16[2,4,10]{2,1,0:T(4,128)(2,1)S(1)}) conditional(s32[]{:T(128)} %convert_element_type.418, (f32[1024,1024]{0,1:T(8,128)}, f32[1024,1024]{0,1:T(8,128)}, f32[1024,1024]{1,0:T(8,128)}) %tuple.54, ...), branch_computations={%region_28.29_spmd, %region_29.31_spmd} | conditional | flops 1347452928 | bytes 63408612 | solution.py:126
  306.5 5.1 %convolution_add_fusion.5 = f32[1024,1024]{1,0:T(8,128)} fusion(f32[1024,1024]{1,0:T(8,128)} %get-tuple-element.149, bf16[80,1024]{1,0:T(8,128)(2,1)S(1)} %copy-done.38, f32[80]{0:T(128)S(1)} %reshape.455, f32[80,1024]{1,0:T(8,128)S(1)} %fusion.104, f32[80,1024]{1,0:T(8,128)S(1)} %fusion.105), kind=kOutput, calls=%fused_computation.44 | convolution fusion | flops 169394176 | bytes 9208128 | tf_op jit(solution)/shard_map/cond/branch_1_fun/dot_general | solution.py:112
  326.5 5.9 %all-to-all-done.15 = bf16[4,10,1024]{2,1,0:T(8,128)(2,1)S(1)} async-done(((bf16[4,10,1024]{2,1,0:T(8,128)(2,1)}), bf16[4,10,1024]{2,1,0:T(8,128)(2,1)S(1)}, u32[]{:S(2)}, u32[]{:S(2)}) %all-to-all-start.15) | async-done | bytes 81952 | tf_op jit(solution)/shard_map/all_to_all | solution.py:137
  337.8 6.9 %all-gather.14 = bf16[8,10,1024]{2,1,0:T(8,128)(2,1)S(1)} all-gather(bf16[4,10,1024]{2,1,0:T(8,128)(2,1)S(1)} %convolution_convert_fusion), channel_id=16, replica_groups=mesh['segment'=4,'expert'=4,'fsdp'=2] {'fsdp'}, dimensions={0}, use_global_device_ids=true | all-gather | bytes 245760 | tf_op jit(solution)/shard_map/all_gather | solution.py:82
  350.8 5.9 %all-gather.12 = bf16[8,10,1024]{2,1,0:T(8,128)(2,1)S(1)} all-gather(bf16[4,10,1024]{2,1,0:T(8,128)(2,1)S(1)} %convolution_convert_fusion.1), channel_id=14, replica_groups=mesh['segment'=4,'expert'=4,'fsdp'=2] {'fsdp'}, dimensions={0}, use_global_device_ids=true | all-gather | bytes 245760 | tf_op jit(solution)/shard_map/all_gather | solution.py:83
  368.4 24.3 %conditional.9 = (f32[1024,1024]{0,1:T(8,128)}, f32[1024,1024]{0,1:T(8,128)}, f32[1024,1024]{1,0:T(8,128)}, bf16[2,4,10,1024]{3,2,1,0:T(8,128)(2,1)S(1)}, bf16[2,4,10]{2,1,0:T(4,128)(2,1)}) conditional(s32[]{:T(128)} %convert_element_type.428, (f32[1024,1024]{0,1:T(8,128)}, f32[1024,1024]{0,1:T(8,128)}, f32[1024,1024]{1,0:T(8,128)}) %tuple.56, ...), branch_computations={%region_36.37_spmd, %region_37.39_spmd} | conditional | flops 1347452928 | bytes 60791012 | solution.py:126
  406.1 7.8 %all-reduce.5 = (bf16[2,4,10]{2,1,0:T(4,128)(2,1)S(1)}, bf16[2,4,10]{2,1,0:T(4,128)(2,1)S(1)}, bf16[2,4,10]{2,1,0:T(4,128)(2,1)S(1)}, bf16[2,4,10]{2,1,0:T(4,128)(2,1)S(1)}, bf16[2,4,10]{2,1,0:T(4,128)(2,1)S(1)}) all-reduce(bf16[2,4,10]{2,1,0:T(4,128)(2,1)S(1)} %copy-done.74, ...), channel_id=26, replica_groups=mesh['segment'=4,'expert'=4,'fsdp'=2] {'fsdp'}, use_global_device_ids=true, to_apply=%region_44.45.clone | all-reduce | flops 400 | bytes 1600
  428.6 5.2 %all-to-all-done.21 = bf16[4,1,10]{2,1,0:T(2,128)(2,1)S(1)} async-done(((bf16[4,1,10]{2,1,0:T(2,128)(2,1)}), bf16[4,1,10]{2,1,0:T(2,128)(2,1)S(1)}, u32[]{:S(2)}, u32[]{:S(2)}) %all-to-all-start.21) | async-done | bytes 112 | tf_op jit(solution)/shard_map/all_to_all | solution.py:144
  437.2 5.2 %all-to-all-done.22 = bf16[4,1,10]{2,1,0:T(2,128)(2,1)S(1)} async-done(((bf16[4,1,10]{2,1,0:T(2,128)(2,1)}), bf16[4,1,10]{2,1,0:T(2,128)(2,1)S(1)}, u32[]{:S(2)}, u32[]{:S(2)}) %all-to-all-start.22) | async-done | bytes 112 | tf_op jit(solution)/shard_map/all_to_all | solution.py:144
  445.8 5.3 %all-to-all-done.23 = bf16[4,1,10]{2,1,0:T(2,128)(2,1)S(1)} async-done(((bf16[4,1,10]{2,1,0:T(2,128)(2,1)}), bf16[4,1,10]{2,1,0:T(2,128)(2,1)S(1)}, u32[]{:S(2)}, u32[]{:S(2)}) %all-to-all-start.23) | async-done | bytes 112 | tf_op jit(solution)/shard_map/all_to_all | solution.py:144
  454.5 5.2 %all-to-all-done.24 = bf16[4,1,10]{2,1,0:T(2,128)(2,1)S(1)} async-done(((bf16[4,1,10]{2,1,0:T(2,128)(2,1)}), bf16[4,1,10]{2,1,0:T(2,128)(2,1)S(1)}, u32[]{:S(2)}, u32[]{:S(2)}) %all-to-all-start.24) | async-done | bytes 112 | tf_op jit(solution)/shard_map/all_to_all | solution.py:144
  464.0 5.2 %all-to-all-done.19 = bf16[4,10,1024]{2,1,0:T(8,128)(2,1)S(1)} async-done(((bf16[4,10,1024]{2,1,0:T(8,128)(2,1)}), bf16[4,10,1024]{2,1,0:T(8,128)(2,1)S(1)}, u32[]{:S(2)}, u32[]{:S(2)}) %all-to-all-start.19) | async-done | bytes 81952 | tf_op jit(solution)/shard_map/all_to_all | solution.py:137
  (366 shorter events, 227.9 us)
Async XLA Ops:
  15.7 14.0 %all-to-all-start.1 = ((bf16[2,4,10]{2,0,1:T(2,128)(2,1)}), bf16[2,4,10]{2,0,1:T(2,128)(2,1)S(1)}, u32[]{:S(2)}, u32[]{:S(2)}) async-start(bf16[2,4,10]{2,0,1:T(2,128)(2,1)} %copy.180), calls=%async_computation.1 | async-start | bytes 4096 | tf_op jit(solution)/shard_map/all_to_all | solution.py:88
  29.7 11.7 %all-to-all-start = ((bf16[2,4,10,1024]{3,0,2,1:T(2,128)(2,1)}), bf16[2,4,10,1024]{3,0,2,1:T(2,128)(2,1)S(1)}, u32[]{:S(2)}, u32[]{:S(2)}) async-start(bf16[2,4,10,1024]{3,0,2,1:T(2,128)(2,1)} %copy.179), calls=%async_computation | async-start | bytes 327680 | tf_op jit(solution)/shard_map/all_to_all | solution.py:87
  41.4 11.1 %all-to-all-start.2 = ((bf16[2,4,10,1024]{3,0,2,1:T(2,128)(2,1)}), bf16[2,4,10,1024]{3,0,2,1:T(2,128)(2,1)S(1)}, u32[]{:S(2)}, u32[]{:S(2)}) async-start(bf16[2,4,10,1024]{3,0,2,1:T(2,128)(2,1)} %copy.182), calls=%async_computation.2 | async-start | bytes 327680 | tf_op jit(solution)/shard_map/all_to_all | solution.py:86
  46.5 31.0 %reduce-scatter.6.cloned.1.call-start = ((), (), s32[]{:S(2)}) async-start(), calls=%async_computation.30 | async-start | bytes 393216 | tf_op jit(solution)/shard_map/reduce_scatter | solution.py:129
  77.5 10.7 %all-to-all-start.3 = ((bf16[4,10,1024]{2,1,0:T(8,128)(2,1)}), bf16[4,10,1024]{2,1,0:T(8,128)(2,1)S(1)}, u32[]{:S(2)}, u32[]{:S(2)}) async-start(bf16[4,10,1024]{2,1,0:T(8,128)(2,1)} %bitcast.344), calls=%async_computation.4 | async-start | bytes 262144 | tf_op jit(solution)/shard_map/all_to_all | solution.py:137
  88.2 13.6 %all-to-all-start.5 = ((bf16[2,4,10]{2,0,1:T(2,128)(2,1)}), bf16[2,4,10]{2,0,1:T(2,128)(2,1)S(1)}, u32[]{:S(2)}, u32[]{:S(2)}) async-start(bf16[2,4,10]{2,0,1:T(2,128)(2,1)} %copy.192), calls=%async_computation.6 | async-start | bytes 4096 | tf_op jit(solution)/shard_map/all_to_all | solution.py:88
  92.3 14.5 %collective-permute-start = (bf16[16,1024]{1,0:T(8,128)(2,1)S(1)}, bf16[16,1024]{1,0:T(8,128)(2,1)S(1)}, u32[]{:S(2)}, u32[]{:S(2)}) collective-permute-start(bf16[16,1024]{1,0:T(8,128)(2,1)S(1)} %fusion.27), channel_id=1, source_target_pairs={{8,0},{16,8},{24,16},{9,1},{17,9},{25,17},{10,2},{18,10},{26,18},{... | collective-permute-start | bytes 98312 | tf_op jit(solution)/shard_map/ppermute | solution.py:10
  101.8 12.1 %all-to-all-start.6 = ((bf16[2,4,10,1024]{3,0,2,1:T(2,128)(2,1)}), bf16[2,4,10,1024]{3,0,2,1:T(2,128)(2,1)S(1)}, u32[]{:S(2)}, u32[]{:S(2)}) async-start(bf16[2,4,10,1024]{3,0,2,1:T(2,128)(2,1)} %copy.194), calls=%async_computation.7 | async-start | bytes 327680 | tf_op jit(solution)/shard_map/all_to_all | solution.py:86
  113.8 10.8 %all-to-all-start.4 = ((bf16[2,4,10,1024]{3,0,2,1:T(2,128)(2,1)}), bf16[2,4,10,1024]{3,0,2,1:T(2,128)(2,1)S(1)}, u32[]{:S(2)}, u32[]{:S(2)}) async-start(bf16[2,4,10,1024]{3,0,2,1:T(2,128)(2,1)} %copy.191), calls=%async_computation.5 | async-start | bytes 327680 | tf_op jit(solution)/shard_map/all_to_all | solution.py:87
  118.6 42.8 %reduce-scatter.8.cloned.1.call-start = ((), (), s32[]{:S(2)}) async-start(), calls=%async_computation.31 | async-start | bytes 393216 | tf_op jit(solution)/shard_map/reduce_scatter | solution.py:129
  161.5 10.7 %all-to-all-start.7 = ((bf16[4,10,1024]{2,1,0:T(8,128)(2,1)}), bf16[4,10,1024]{2,1,0:T(8,128)(2,1)S(1)}, u32[]{:S(2)}, u32[]{:S(2)}) async-start(bf16[4,10,1024]{2,1,0:T(8,128)(2,1)} %bitcast.347), calls=%async_computation.9 | async-start | bytes 262144 | tf_op jit(solution)/shard_map/all_to_all | solution.py:137
  172.1 12.5 %all-to-all-start.9 = ((bf16[2,4,10]{2,0,1:T(2,128)(2,1)}), bf16[2,4,10]{2,0,1:T(2,128)(2,1)S(1)}, u32[]{:S(2)}, u32[]{:S(2)}) async-start(bf16[2,4,10]{2,0,1:T(2,128)(2,1)} %copy.204), calls=%async_computation.11 | async-start | bytes 4096 | tf_op jit(solution)/shard_map/all_to_all | solution.py:88
  175.6 14.1 %collective-permute-start.1 = (bf16[16,1024]{1,0:T(8,128)(2,1)S(1)}, bf16[16,1024]{1,0:T(8,128)(2,1)S(1)}, u32[]{:S(2)}, u32[]{:S(2)}) collective-permute-start(bf16[16,1024]{1,0:T(8,128)(2,1)S(1)} %add_convert_fusion.3), channel_id=1, source_target_pairs={{8,0},{16,8},{24,16},{9,1},{17,9},{25,17},{10,2},{18,10},{26,18},{... | collective-permute-start | bytes 98312 | tf_op jit(solution)/shard_map/ppermute | solution.py:10
  184.6 12.0 %all-to-all-start.10 = ((bf16[2,4,10,1024]{3,0,2,1:T(2,128)(2,1)}), bf16[2,4,10,1024]{3,0,2,1:T(2,128)(2,1)S(1)}, u32[]{:S(2)}, u32[]{:S(2)}) async-start(bf16[2,4,10,1024]{3,0,2,1:T(2,128)(2,1)} %copy.206), calls=%async_computation.12 | async-start | bytes 327680 | tf_op jit(solution)/shard_map/all_to_all | solution.py:86
  196.6 10.8 %all-to-all-start.8 = ((bf16[2,4,10,1024]{3,0,2,1:T(2,128)(2,1)}), bf16[2,4,10,1024]{3,0,2,1:T(2,128)(2,1)S(1)}, u32[]{:S(2)}, u32[]{:S(2)}) async-start(bf16[2,4,10,1024]{3,0,2,1:T(2,128)(2,1)} %copy.203), calls=%async_computation.10 | async-start | bytes 327680 | tf_op jit(solution)/shard_map/all_to_all | solution.py:87
  201.4 41.3 %reduce-scatter.10.cloned.1.call-start = ((), (), s32[]{:S(2)}) async-start(), calls=%async_computation.32 | async-start | bytes 393216 | tf_op jit(solution)/shard_map/reduce_scatter | solution.py:129
  242.7 10.7 %all-to-all-start.11 = ((bf16[4,10,1024]{2,1,0:T(8,128)(2,1)}), bf16[4,10,1024]{2,1,0:T(8,128)(2,1)S(1)}, u32[]{:S(2)}, u32[]{:S(2)}) async-start(bf16[4,10,1024]{2,1,0:T(8,128)(2,1)} %bitcast.346), calls=%async_computation.14 | async-start | bytes 262144 | tf_op jit(solution)/shard_map/all_to_all | solution.py:137
  253.4 12.5 %all-to-all-start.13 = ((bf16[2,4,10]{2,0,1:T(2,128)(2,1)}), bf16[2,4,10]{2,0,1:T(2,128)(2,1)S(1)}, u32[]{:S(2)}, u32[]{:S(2)}) async-start(bf16[2,4,10]{2,0,1:T(2,128)(2,1)} %copy.216), calls=%async_computation.16 | async-start | bytes 4096 | tf_op jit(solution)/shard_map/all_to_all | solution.py:88
  256.8 14.1 %collective-permute-start.2 = (bf16[16,1024]{1,0:T(8,128)(2,1)S(1)}, bf16[16,1024]{1,0:T(8,128)(2,1)S(1)}, u32[]{:S(2)}, u32[]{:S(2)}) collective-permute-start(bf16[16,1024]{1,0:T(8,128)(2,1)S(1)} %add_convert_fusion.2), channel_id=1, source_target_pairs={{8,0},{16,8},{24,16},{9,1},{17,9},{25,17},{10,2},{18,10},{26,18},{... | collective-permute-start | bytes 98312 | tf_op jit(solution)/shard_map/ppermute | solution.py:10
  265.8 12.2 %all-to-all-start.14 = ((bf16[2,4,10,1024]{3,0,2,1:T(2,128)(2,1)}), bf16[2,4,10,1024]{3,0,2,1:T(2,128)(2,1)S(1)}, u32[]{:S(2)}, u32[]{:S(2)}) async-start(bf16[2,4,10,1024]{3,0,2,1:T(2,128)(2,1)} %copy.218), calls=%async_computation.17 | async-start | bytes 327680 | tf_op jit(solution)/shard_map/all_to_all | solution.py:86
  278.1 10.8 %all-to-all-start.12 = ((bf16[2,4,10,1024]{3,0,2,1:T(2,128)(2,1)}), bf16[2,4,10,1024]{3,0,2,1:T(2,128)(2,1)S(1)}, u32[]{:S(2)}, u32[]{:S(2)}) async-start(bf16[2,4,10,1024]{3,0,2,1:T(2,128)(2,1)} %copy.215), calls=%async_computation.15 | async-start | bytes 327680 | tf_op jit(solution)/shard_map/all_to_all | solution.py:87
  282.9 38.7 %reduce-scatter.12.cloned.1.call-start = ((), (), s32[]{:S(2)}) async-start(), calls=%async_computation.33 | async-start | bytes 393216 | tf_op jit(solution)/shard_map/reduce_scatter | solution.py:129
  321.7 10.7 %all-to-all-start.15 = ((bf16[4,10,1024]{2,1,0:T(8,128)(2,1)}), bf16[4,10,1024]{2,1,0:T(8,128)(2,1)S(1)}, u32[]{:S(2)}, u32[]{:S(2)}) async-start(bf16[4,10,1024]{2,1,0:T(8,128)(2,1)} %bitcast.345), calls=%async_computation.19 | async-start | bytes 262144 | tf_op jit(solution)/shard_map/all_to_all | solution.py:137
  332.3 13.2 %all-to-all-start.17 = ((bf16[2,4,10]{2,0,1:T(2,128)(2,1)}), bf16[2,4,10]{2,0,1:T(2,128)(2,1)S(1)}, u32[]{:S(2)}, u32[]{:S(2)}) async-start(bf16[2,4,10]{2,0,1:T(2,128)(2,1)} %copy.228), calls=%async_computation.21 | async-start | bytes 4096 | tf_op jit(solution)/shard_map/all_to_all | solution.py:88
  336.5 14.1 %collective-permute-start.3 = (bf16[16,1024]{1,0:T(8,128)(2,1)S(1)}, bf16[16,1024]{1,0:T(8,128)(2,1)S(1)}, u32[]{:S(2)}, u32[]{:S(2)}) collective-permute-start(bf16[16,1024]{1,0:T(8,128)(2,1)S(1)} %add_convert_fusion.1), channel_id=1, source_target_pairs={{8,0},{16,8},{24,16},{9,1},{17,9},{25,17},{10,2},{18,10},{26,18},{... | collective-permute-start | bytes 98312 | tf_op jit(solution)/shard_map/ppermute | solution.py:10
  345.6 12.0 %all-to-all-start.18 = ((bf16[2,4,10,1024]{3,0,2,1:T(2,128)(2,1)}), bf16[2,4,10,1024]{3,0,2,1:T(2,128)(2,1)S(1)}, u32[]{:S(2)}, u32[]{:S(2)}) async-start(bf16[2,4,10,1024]{3,0,2,1:T(2,128)(2,1)} %copy.230), calls=%async_computation.22 | async-start | bytes 327680 | tf_op jit(solution)/shard_map/all_to_all | solution.py:86
  357.6 10.8 %all-to-all-start.16 = ((bf16[2,4,10,1024]{3,0,2,1:T(2,128)(2,1)}), bf16[2,4,10,1024]{3,0,2,1:T(2,128)(2,1)S(1)}, u32[]{:S(2)}, u32[]{:S(2)}) async-start(bf16[2,4,10,1024]{3,0,2,1:T(2,128)(2,1)} %copy.227), calls=%async_computation.20 | async-start | bytes 327680 | tf_op jit(solution)/shard_map/all_to_all | solution.py:87
  418.4 41.6 %reduce-scatter.14.cloned.1.call-start = ((), (), s32[]{:S(2)}) async-start(), calls=%async_computation.34 | async-start | bytes 393216 | tf_op jit(solution)/shard_map/reduce_scatter | solution.py:129
  423.7 10.0 %all-to-all-start.21 = ((bf16[4,1,10]{2,1,0:T(2,128)(2,1)}), bf16[4,1,10]{2,1,0:T(2,128)(2,1)S(1)}, u32[]{:S(2)}, u32[]{:S(2)}) async-start(bf16[4,1,10]{2,1,0:T(2,128)(2,1)} %copy.236), calls=%async_computation.26 | async-start | bytes 4096 | tf_op jit(solution)/shard_map/all_to_all | solution.py:144
  442.4 8.7 %all-to-all-start.23 = ((bf16[4,1,10]{2,1,0:T(2,128)(2,1)}), bf16[4,1,10]{2,1,0:T(2,128)(2,1)S(1)}, u32[]{:S(2)}, u32[]{:S(2)}) async-start(bf16[4,1,10]{2,1,0:T(2,128)(2,1)} %copy.238), calls=%async_computation.28 | async-start | bytes 4096 | tf_op jit(solution)/shard_map/all_to_all | solution.py:144
  451.1 8.7 %all-to-all-start.24 = ((bf16[4,1,10]{2,1,0:T(2,128)(2,1)}), bf16[4,1,10]{2,1,0:T(2,128)(2,1)S(1)}, u32[]{:S(2)}, u32[]{:S(2)}) async-start(bf16[4,1,10]{2,1,0:T(2,128)(2,1)} %copy.239), calls=%async_computation.29 | async-start | bytes 4096 | tf_op jit(solution)/shard_map/all_to_all | solution.py:144
  459.9 9.2 %all-to-all-start.19 = ((bf16[4,10,1024]{2,1,0:T(8,128)(2,1)}), bf16[4,10,1024]{2,1,0:T(8,128)(2,1)S(1)}, u32[]{:S(2)}, u32[]{:S(2)}) async-start(bf16[4,10,1024]{2,1,0:T(8,128)(2,1)} %bitcast.343), calls=%async_computation.24 | async-start | bytes 262144 | tf_op jit(solution)/shard_map/all_to_all | solution.py:137
  (75 other events, 1993.7 us)
Sparse Core Ops, SparseCore 0:
  61.2 16.2 reduce-scatter.5
  125.7 35.6 reduce-scatter.7
  208.4 34.2 reduce-scatter.9
  312.4 9.1 reduce-scatter.11
  423.5 12.0 reduce-scatter.13
where the time goes:
time: 480 us; the launch traced here: 477 us
  waiting for transfers between devices  149 us (31%)
  starting transfers between devices  113 us (24%)
  blocking collectives  92.9 us (19%)
  local copies, waits for them, and re-layouts  48 us (10%)
  matrix products  47.3 us (10%)
  between operations  14.6 us (3%)
  other arithmetic  10.8 us (2%)
    reduce_scatter x5, waiting for transfers between devices, local(): lax.psum_scatter(part_rows, 'fsdp', scatter_dimension=0, tiled=True)  87.5 us
    all_gather x5, blocking collectives, local(): lax.all_gather(token_buf[None], 'fsdp', axis=0, tiled=True)  33.2 us
    all_gather x5, blocking collectives, local(): lax.all_gather(grad_buf[None], 'fsdp', axis=0, tiled=True)  29.5 us
    all_to_all x5, starting transfers between devices, local(): lax.all_to_all(grouped[0], 'expert', split_axis=1, concat_axis=1, tiled=T...  25.4 us
    all_to_all x5, starting transfers between devices, local(): lax.all_to_all(grouped[1], 'expert', split_axis=1, concat_axis=1, tiled=T...  24.4 us
    all_to_all x5, waiting for transfers between devices, local(): lax.all_to_all(summed_rows[0].astype(jnp.bfloat16), 'expert', split_axis=...  23.7 us
    all_gather x5, blocking collectives, local(): lax.all_gather(gate_buf[None], 'fsdp', axis=0, tiled=True)  22.4 us
    all_to_all x5, starting transfers between devices, local(): lax.all_to_all(summed_rows[0].astype(jnp.bfloat16), 'expert', split_axis=...  21.7 us
  transfers between devices with their start and end apart: 34, of which 19 were waited for; matrix products, arithmetic and copies ran while one was open for 6% of the time, Pallas kernels for 0%

commit v1 on v0

--- a/solution.py
+++ b/solution.py
@@ -1,7 +1,327 @@
+import functools
+
 import jax
 import jax.numpy as jnp
 from jax import lax
+from jax.experimental import pallas as pl
+from jax.experimental.pallas import tpu as pltpu
 from jax.sharding import PartitionSpec as P
+
+MESH = pl.DeviceIdType.MESH
+LANES = 128
+ROWS = 16
+TILE = 256
+ROOM = 44 << 20
+CONTRACT_ROWS = (((0,), (0,)), ((), ()))
+CONTRACT_COLS = (((1,), (1,)), ((), ()))
+
+
+def relay_kernel(
+    segments, n_expert, n_fsdp,
+    acts, out_grad, ids, gates, w_gate, w_up, w_down,
+    act_out, gate_out, x_out, g_out, da_out, db_out, hg_out,
+    wg, wu, wd, xbuf, gbuf, rbuf, zbuf, rst, zst, newg,
+    slope_buf, act_buf, hid_buf, da, db, hg,
+    w_sem, out_sem, xs, xr, os, gr, ds, rs, rr, zs, zr,
+):
+    group = n_expert * n_fsdp
+    micros, toks, width = acts.shape[1:]
+    hid = wg.shape[1]
+    rows = group * toks
+    last = segments - 1
+    seg = lax.axis_index("segment")
+    expert = lax.axis_index("expert")
+    me = expert * n_fsdp + lax.axis_index("fsdp")
+    is_last = seg == last
+    tiles = [(s, min(TILE, hid - s)) for s in range(0, hid, TILE)]
+    d_tiles = [(s, min(TILE, width - s)) for s in range(0, width, TILE)]
+
+    def at(layer, member):
+        return (layer, member // n_fsdp, member % n_fsdp)
+
+    def others(fn):
+        def body(i, carry):
+            fn((me + i) % group)
+            return carry
+        lax.fori_loop(1, group, body, 0)
+
+    def members(fn):
+        def body(i, carry):
+            fn((me + i) % group)
+            return carry
+        lax.fori_loop(0, group, body, 0)
+
+    loads = [
+        pltpu.make_async_copy(src.at[0, 0], dst, w_sem.at[i])
+        for i, (src, dst) in enumerate(((w_gate, wg), (w_up, wu), (w_down, wd)))
+    ]
+    for load in loads:
+        load.start()
+
+    barrier = pltpu.get_barrier_semaphore()
+
+    def greet(layer):
+        def go(j):
+            pl.semaphore_signal(barrier, inc=1, device_id=at(layer, j), device_id_type=MESH)
+        return go
+
+    others(greet(seg))
+
+    @pl.when(seg > 0)
+    def _():
+        members(greet(seg - 1))
+
+    @pl.when(seg < last)
+    def _():
+        members(greet(seg + 1))
+
+    lane = lax.broadcasted_iota(jnp.int32, (toks, LANES), 1)
+    for m in range(micros):
+        xbuf[m, me, :, :width] = acts[0, m]
+        named = ids[0, m]
+        weight = gates[0, m].astype(jnp.float32)
+        spread = jnp.zeros((toks, LANES), jnp.float32)
+        for k in range(named.shape[1]):
+            spread = spread + jnp.where(named[:, k : k + 1] == lane, weight[:, k : k + 1], 0.0)
+        xbuf[m, me, :, width:] = spread.astype(jnp.bfloat16)
+
+    @pl.when(is_last)
+    def _():
+        for m in range(micros):
+            gbuf[m, me] = out_grad[m]
+
+    below, above = (seg + last) // segments, (2 * last - seg) // segments
+    pl.semaphore_wait(barrier, group - 1 + group * below + group * above)
+
+    def x_copy(m, block, j):
+        return pltpu.make_async_remote_copy(
+            xbuf.at[m, block], xbuf.at[m, block], xs.at[m, j], xr.at[m, block],
+            device_id=at(seg, j), device_id_type=MESH)
+
+    def own_copy(m, block, j):
+        return pltpu.make_async_remote_copy(
+            gbuf.at[m, block], gbuf.at[m, block], os.at[m, j], gr.at[m, block],
+            device_id=at(seg, j), device_id_type=MESH)
+
+    def down_copy(m, block, j):
+        return pltpu.make_async_remote_copy(
+            newg.at[m], gbuf.at[m, block], ds.at[m, j], gr.at[m, block],
+            device_id=at(lax.max(seg - 1, 0), j), device_id_type=MESH)
+
+    def r_copy(m, block, j):
+        return pltpu.make_async_remote_copy(
+            rst.at[m, j], rbuf.at[m, block], rs.at[m, j], rr.at[m, block],
+            device_id=at(seg, j), device_id_type=MESH)
+
+    def z_copy(block, j):
+        return pltpu.make_async_remote_copy(
+            zst.at[j], zbuf.at[block], zs.at[j], zr.at[block],
+            device_id=at(seg, j), device_id_type=MESH)
+
+    for m in range(micros):
+        others(lambda j: x_copy(m, me, j).start())
+
+        @pl.when(is_last)
+        def _():
+            others(lambda j: own_copy(m, me, j).start())
+
+    stores = []
+
+    def keep(src, dst):
+        copy = pltpu.make_async_copy(src, dst, out_sem.at[len(stores)])
+        copy.start()
+        stores.append(copy)
+
+    def prepare(m):
+        others(lambda j: x_copy(m, j, j).wait_recv())
+        x = xbuf[m, :, :, :width].reshape(rows, width)
+        weights = xbuf[m, :, :, width:].reshape(rows, LANES).astype(jnp.float32)
+        mine = lax.broadcasted_iota(jnp.int32, (rows, LANES), 1) == expert
+        c = jnp.sum(jnp.where(mine, weights, 0.0), axis=1, keepdims=True)
+        for s, size in tiles:
+            cut = slice(s, s + size)
+            a = jnp.dot(x, wg[:, cut], preferred_element_type=jnp.float32)
+            b = jnp.dot(x, wu[:, cut], preferred_element_type=jnp.float32)
+            sigmoid = jax.nn.sigmoid(a)
+            silu = a * sigmoid
+            hidden = silu * b
+            slope_buf[m, :, cut] = c * b * (sigmoid * (1.0 + a * (1.0 - sigmoid)))
+            act_buf[m, :, cut] = c * silu
+            hid_buf[m, :, cut] = hidden
+            hg[m, :, cut] = (hidden * c).astype(jnp.bfloat16)
+
+    def partial(m):
+        others(lambda j: own_copy(m, j, j).wait_recv())
+
+        @pl.when(seg < last)
+        def _():
+            own_copy(m, me, me).wait_recv()
+
+        g = gbuf[m].reshape(rows, width)
+        z = jnp.zeros((rows, 1), jnp.float32)
+        for s, size in tiles:
+            cut = slice(s, s + size)
+            q = lax.dot_general(g, wd[cut, :], CONTRACT_COLS, preferred_element_type=jnp.float32)
+            da[m, :, cut] = (q * slope_buf[m, :, cut]).astype(jnp.bfloat16)
+            db[m, :, cut] = (q * act_buf[m, :, cut]).astype(jnp.bfloat16)
+            z = z + jnp.sum(q * hid_buf[m, :, cut], axis=1, keepdims=True)
+        for s, size in d_tiles:
+            cut = slice(s, s + size)
+            r = lax.dot_general(da[m], wg[cut, :], CONTRACT_COLS, preferred_element_type=jnp.float32)
+            r = r + lax.dot_general(db[m], wu[cut, :], CONTRACT_COLS, preferred_element_type=jnp.float32)
+            rst[m, :, :, cut] = r.astype(jnp.bfloat16).reshape(group, toks, size)
+        rbuf[m, me] = rst[m, me]
+        others(lambda j: r_copy(m, me, j).start())
+        zst[:, m] = jnp.broadcast_to(z, (rows, LANES)).astype(jnp.bfloat16).reshape(group, toks, LANES)
+
+    def combine(m):
+        others(lambda j: r_copy(m, j, j).wait_recv())
+        total = gbuf[m, me].astype(jnp.float32)
+        for e in range(n_expert):
+            part = rbuf[m, e * n_fsdp].astype(jnp.float32)
+            for f in range(1, n_fsdp):
+                part = part + rbuf[m, e * n_fsdp + f].astype(jnp.float32)
+            total = total + part.astype(jnp.bfloat16).astype(jnp.float32)
+        fresh = total.astype(jnp.bfloat16)
+        newg[m] = fresh
+
+        @pl.when(seg > 0)
+        def _():
+            members(lambda j: down_copy(m, me, j).start())
+
+        act_out[0, m] = fresh
+
+    for load in loads:
+        load.wait()
+    prepare(0)
+
+    @pl.when(seg < last)
+    def _():
+        for m in range(1, micros):
+            prepare(m)
+
+    for m in range(micros):
+        if m > 0:
+            @pl.when(is_last)
+            def _():
+                prepare(m)
+        partial(m)
+    for m in range(micros):
+        combine(m)
+
+    zbuf[me] = zst[me]
+    others(lambda j: z_copy(me, j).start())
+    for m in range(micros):
+        keep(xbuf.at[m, :, :, pl.ds(0, width)], x_out.at[m])
+        keep(gbuf.at[m], g_out.at[m])
+        keep(da.at[m], da_out.at[m])
+        keep(db.at[m], db_out.at[m])
+        keep(hg.at[m], hg_out.at[m])
+    others(lambda j: z_copy(j, j).wait_recv())
+    for m in range(micros):
+        named = ids[0, m]
+        total = jnp.zeros(named.shape, jnp.float32)
+        for e in range(n_expert):
+            part = zbuf[e * n_fsdp, m].astype(jnp.float32)
+            for f in range(1, n_fsdp):
+                part = part + zbuf[e * n_fsdp + f, m].astype(jnp.float32)
+            part = part.astype(jnp.bfloat16).astype(jnp.float32)
+            total = total + jnp.where(named == e, part[:, : named.shape[1]], 0.0)
+        gate_out[0, m] = total
+
+    for m in range(micros):
+        others(lambda j: x_copy(m, me, j).wait_send())
+        others(lambda j: r_copy(m, me, j).wait_send())
+
+        @pl.when(is_last)
+        def _():
+            others(lambda j: own_copy(m, me, j).wait_send())
+
+        @pl.when(seg > 0)
+        def _():
+            members(lambda j: down_copy(m, me, j).wait_send())
+    others(lambda j: z_copy(me, j).wait_send())
+    for copy in stores:
+        copy.wait()
+
+
+def relay_room(acts, w_gate, group):
+    micros, toks, width = acts.shape[1:]
+    hid = w_gate.shape[3]
+    rows = micros * group * toks
+    return 3 * width * hid * 2 + rows * (width * 2 * 4 + hid * (3 * 4 + 3 * 2) + LANES * 6)
+
+
+def relay(acts, out_grad, ids, gates, w_gate, w_up, w_down):
+    segments = lax.axis_size("segment")
+    n_expert = lax.axis_size("expert")
+    n_fsdp = lax.axis_size("fsdp")
+    group = n_expert * n_fsdp
+    micros, toks, width = acts.shape[1:]
+    hid = w_gate.shape[3]
+    fits = (
+        toks % ROWS == 0
+        and width % LANES == 0
+        and hid % LANES == 0
+        and n_expert <= LANES
+        and relay_room(acts, w_gate, group) <= ROOM
+    )
+    if not fits:
+        return local(acts, out_grad, ids, gates, w_gate, w_up, w_down)
+    rows = group * toks
+    bf16, f32 = jnp.bfloat16, jnp.float32
+    vmem = pl.BlockSpec(memory_space=pltpu.VMEM)
+    far = pl.BlockSpec(memory_space=pl.ANY)
+    dma = pltpu.SemaphoreType.DMA
+    scratch = [
+        pltpu.VMEM((width, hid), bf16),
+        pltpu.VMEM((width, hid), bf16),
+        pltpu.VMEM((hid, width), bf16),
+        pltpu.VMEM((micros, group, toks, width + LANES), bf16),
+        pltpu.VMEM((micros, group, toks, width), bf16),
+        pltpu.VMEM((micros, group, toks, width), bf16),
+        pltpu.VMEM((group, micros, toks, LANES), bf16),
+        pltpu.VMEM((micros, group, toks, width), bf16),
+        pltpu.VMEM((group, micros, toks, LANES), bf16),
+        pltpu.VMEM((micros, toks, width), bf16),
+    ]
+    scratch += [pltpu.VMEM((micros, rows, hid), f32)] * 3
+    scratch += [pltpu.VMEM((micros, rows, hid), bf16)] * 3
+    scratch += [dma((3,)), dma((5 * micros,))]
+    scratch += [dma((micros, group))] * 7
+    scratch += [dma((group,))] * 2
+    flops = 2 * micros * rows * width * hid * 5
+    outs = pl.pallas_call(
+        functools.partial(relay_kernel, segments, n_expert, n_fsdp),
+        out_shape=(
+            jax.ShapeDtypeStruct(acts.shape, bf16),
+            jax.ShapeDtypeStruct(gates.shape, f32),
+            jax.ShapeDtypeStruct((micros, group, toks, width), bf16),
+            jax.ShapeDtypeStruct((micros, group, toks, width), bf16),
+            jax.ShapeDtypeStruct((micros, rows, hid), bf16),
+            jax.ShapeDtypeStruct((micros, rows, hid), bf16),
+            jax.ShapeDtypeStruct((micros, rows, hid), bf16),
+        ),
+        in_specs=[vmem, vmem, vmem, vmem, far, far, far],
+        out_specs=(vmem, vmem, far, far, far, far, far),
+        scratch_shapes=scratch,
+        compiler_params=pltpu.CompilerParams(
+            collective_id=0, has_side_effects=True, vmem_limit_bytes=ROOM + (8 << 20)
+        ),
+        cost_estimate=pl.CostEstimate(
+            flops=flops, bytes_accessed=6 * width * hid, transcendentals=micros * rows * hid
+        ),
+    )(acts, out_grad, ids, gates, w_gate, w_up, w_down)
+    act_grad, gate_grad, x, g, da, db, hg = outs
+    x = x.reshape(-1, width)
+    g = g.reshape(-1, width)
+
+    def weight_grad(left, right):
+        total = lax.dot_general(left, right, CONTRACT_ROWS, preferred_element_type=f32)
+        return total.astype(bf16)[None, None]
+
+    da, db, hg = (v.reshape(-1, hid) for v in (da, db, hg))
+    return act_grad, gate_grad, weight_grad(x, da), weight_grad(x, db), weight_grad(hg, g)
 
 
 def from_behind(value, axis, steps):
@@ -184,4 +504,4 @@
         P("segment", "expert", None, "fsdp"),
         P("segment", "expert", "fsdp", None),
     )
-    return jax.shard_map(local, mesh=mesh, in_specs=in_specs, out_specs=out_specs, check_vma=False)
+    return jax.shard_map(relay, mesh=mesh, in_specs=in_specs, out_specs=out_specs, check_vma=False)

time: 480 us -> 94.7 us (0.20)
  waiting for transfers between devices: 149 us -> 0 us
  starting transfers between devices: 113 us -> 0 us
  blocking collectives: 92.9 us -> 0 us
  Pallas kernels: 0 us -> 82 us
  local copies, waits for them, and re-layouts: 48 us -> 4.51 us
  matrix products: 47.3 us -> 7.24 us
  between operations: 14.6 us -> 0.65 us
  other arithmetic: 10.8 us -> 0 us
    all_to_all x25 -> x0, starting transfers between devices: 108 us -> none  [the longest x5 25.4 us: local(): lax.all_to_all(grouped[0], 'expert', split_axis=1, concat_axis=1, tiled=T...]
    reduce_scatter x5 -> x0, waiting for transfers between devices: 87.5 us -> none  [local(): lax.psum_scatter(part_rows, 'fsdp', scatter_dimension=0, tiled=True)]
    all_gather x15 -> x0, blocking collectives: 85.1 us -> none  [the longest x5 33.2 us: local(): lax.all_gather(token_buf[None], 'fsdp', axis=0, tiled=True)]
    pallas_call x0 -> x1, Pallas kernels: none -> 82 us  [relay(): pl.pallas_call(functools.partial(relay_kernel, segments, n_expert, n_fsdp...]
    all_to_all x25 -> x0, waiting for transfers between devices: 61.8 us -> none  [the longest x5 23.7 us: local(): lax.all_to_all(summed_rows[0].astype(jnp.bfloat16), 'expert', split_axis=...]
    dot_general x41 -> x3, matrix products: 47.3 us -> 7.24 us  [weight_grad(): lax.dot_general(left, right, CONTRACT_ROWS, preferred_element_type=f32)]
    cond x38 -> x0, local copies, waits for them, and re-layouts: 12.9 us -> none  [the longest x2 9.3 us: local(): finished = lax.cond(valid, compute, lambda state: state, start_state)]
    all_gather x15 -> x0, local copies, waits for them, and re-layouts: 12.6 us -> none  [the longest x5 4.26 us: local(): lax.all_gather(gate_buf[None], 'fsdp', axis=0, tiled=True)]
  transfers between devices with their start and end apart: 34 -> 0, of which waited for: 19 -> 0; matrix products, arithmetic and copies ran while one was open for 6% -> 0% of each run, Pallas kernels for 0% -> 0%
where the time goes in v1:
time: 94.7 us; the launch traced here: 94.4 us
  Pallas kernels  82 us (87%)
  matrix products  7.24 us (8%)
  local copies, waits for them, and re-layouts  4.51 us (5%)
    pallas_call x1, Pallas kernels, relay(): pl.pallas_call(functools.partial(relay_kernel, segments, n_expert, n_fsdp...  82 us
    dot_general x3, matrix products, weight_grad(): lax.dot_general(left, right, CONTRACT_ROWS, preferred_element_type=f32)  7.24 us
    unnamed x10, local copies, waits for them, and re-layouts  4.51 us

profile of v1, /device:TPU:0, one launch (start us, length us, event | category | flops | bytes accessed | tf_op | source)
XLA Modules:
  0.0 94.4 jit_solution(14110973223661739730)
XLA Ops:
  0.6 0.8 copy.13.gates
  1.4 0.8 copy.12.ids
  2.2 0.0 copy-start
  2.2 0.8 copy-done
  3.0 0.0 copy-start.1
  3.0 0.8 copy-done.1
  3.9 82.0 %shard_map.110 = (bf16[1,2,16,1024]{3,2,1,0:T(8,128)(2,1)S(1)}, f32[1,2,16,2]{3,2,1,0:T(8,128)S(1)}, bf16[2,8,16,1024]{3,2,1,0:T(8,128)(2,1)S(1)}, bf16[2,8,16,1...) custom-call(bf16[1,2,16,1024]{3,2,1,0:T(8,128)(2,1)S(1)} %copy-done,, ...), custom_call_target="tpu_custom_call" | custom-call | flops 2684354560 | bytes 6291456 | tf_op jit(solution)/shard_map/pallas_call | solution.py:294
  85.9 0.7 copy.14
  86.5 3.1 %convert_bitcast_fusion.1 = bf16[1,1,1024,1024]{3,2,1,0:T(8,128)(2,1)} fusion(bf16[256,1024]{1,0:T(8,128)(2,1)S(1)} %bitcast.17, bf16[256,1024]{1,0:T(8,128)(2,1)} %bitcast.22), kind=kOutput, calls=%fused_computation.1 | convolution fusion | flops 537919488 | bytes 3145728 | tf_op jit(solution)/shard_map/dot_general | solution.py:320
  89.7 0.0 copy-start.2
  89.7 2.1 %convert_bitcast_fusion.2 = bf16[1,1,1024,1024]{3,2,1,0:T(8,128)(2,1)} fusion(bf16[256,1024]{1,0:T(8,128)(2,1)S(1)} %bitcast.18, bf16[256,1024]{1,0:T(8,128)(2,1)S(1)} %bitcast.20), kind=kOutput, calls=%fused_computation.2 | convolution fusion | flops 537919488 | bytes 3145728 | tf_op jit(solution)/shard_map/dot_general | solution.py:320
  91.7 0.0 copy-done.2
  91.7 2.1 %convert_bitcast_fusion = bf16[1,1,1024,1024]{3,2,1,0:T(8,128)(2,1)} fusion(bf16[256,1024]{1,0:T(8,128)(2,1)S(1)} %bitcast.21, bf16[256,1024]{1,0:T(8,128)(2,1)S(1)} %bitcast.19), kind=kOutput, calls=%fused_computation | convolution fusion | flops 537919488 | bytes 3145728 | tf_op jit(solution)/shard_map/dot_general | solution.py:320
  93.8 0.6 copy.16
Async XLA Ops:
  2.2 0.8 copy-start
  3.0 0.8 copy-start.1
  89.7 2.1 %copy-start.2 = (bf16[2,128,1024]{2,1,0:T(8,128)(2,1)S(1)}, bf16[2,128,1024]{2,1,0:T(8,128)(2,1)}, u32[]{:S(2)}) copy-start(bf16[2,128,1024]{2,1,0:T(8,128)(2,1)} %get-tuple-element.17) | copy-start | bytes 1572868

commit v2 on v1

--- a/solution.py
+++ b/solution.py
@@ -11,48 +11,76 @@
 LANES = 128
 ROWS = 16
 TILE = 256
+GRANT = 62 << 20
 ROOM = 44 << 20
-CONTRACT_ROWS = (((0,), (0,)), ((), ()))
+PARTS = 2
 CONTRACT_COLS = (((1,), (1,)), ((), ()))
 
 
 def relay_kernel(
     segments, n_expert, n_fsdp,
     acts, out_grad, ids, gates, w_gate, w_up, w_down,
-    act_out, gate_out, x_out, g_out, da_out, db_out, hg_out,
+    act_out, gate_out, xt_out, g_out, da_out, db_out, hgt_out,
     wg, wu, wd, xbuf, gbuf, rbuf, zbuf, rst, zst, newg,
-    slope_buf, act_buf, hid_buf, da, db, hg,
-    w_sem, out_sem, xs, xr, os, gr, ds, rs, rr, zs, zr,
+    slope_buf, act_buf, hid_buf, qbuf, da, db, hg, xt, hgt,
+    in_sem, out_sem, go, xs, xr, os, gr, ds, rs, rr, zs, zr,
 ):
     group = n_expert * n_fsdp
     micros, toks, width = acts.shape[1:]
     hid = wg.shape[1]
     rows = group * toks
     last = segments - 1
+    part_width = newg.shape[2]
+    parts = width // part_width
     seg = lax.axis_index("segment")
     expert = lax.axis_index("expert")
-    me = expert * n_fsdp + lax.axis_index("fsdp")
+    fsdp = lax.axis_index("fsdp")
+    me = expert * n_fsdp + fsdp
     is_last = seg == last
     tiles = [(s, min(TILE, hid - s)) for s in range(0, hid, TILE)]
-    d_tiles = [(s, min(TILE, width - s)) for s in range(0, width, TILE)]
+    d_tiles = [(s, min(TILE, part_width - s)) for s in range(0, part_width, TILE)]
 
     def at(layer, member):
         return (layer, member // n_fsdp, member % n_fsdp)
 
+    def turn_round(first, count, start, fn):
+        def body(i, carry):
+            fn((start + i) % count)
+            return carry
+        lax.fori_loop(first, count, body, 0)
+
     def others(fn):
-        def body(i, carry):
-            fn((me + i) % group)
-            return carry
-        lax.fori_loop(1, group, body, 0)
+        turn_round(1, group, me, fn)
 
     def members(fn):
-        def body(i, carry):
-            fn((me + i) % group)
-            return carry
-        lax.fori_loop(0, group, body, 0)
+        turn_round(0, group, me, fn)
+
+    def other_experts(fn):
+        turn_round(1, n_expert, expert, fn)
+
+    def other_fsdp(fn):
+        turn_round(1, n_fsdp, fsdp, fn)
+
+    def own_loss(m, c):
+        return pltpu.make_async_copy(
+            out_grad.at[m, :, pl.ds(c * part_width, part_width)], gbuf.at[m * parts + c, me],
+            in_sem.at[3 + micros + m * parts + c])
+
+    own_acts = [
+        pltpu.make_async_copy(acts.at[0, m], xbuf.at[m, me, :, pl.ds(0, width)], in_sem.at[3 + m])
+        for m in range(micros)
+    ]
+    for copy in own_acts:
+        copy.start()
+
+    @pl.when(is_last)
+    def _():
+        for m in range(micros):
+            for c in range(parts):
+                own_loss(m, c).start()
 
     loads = [
-        pltpu.make_async_copy(src.at[0, 0], dst, w_sem.at[i])
+        pltpu.make_async_copy(src.at[0, 0], dst, in_sem.at[i])
         for i, (src, dst) in enumerate(((w_gate, wg), (w_up, wu), (w_down, wd)))
     ]
     for load in loads:
@@ -61,9 +89,9 @@
     barrier = pltpu.get_barrier_semaphore()
 
     def greet(layer):
-        def go(j):
+        def tell(j):
             pl.semaphore_signal(barrier, inc=1, device_id=at(layer, j), device_id_type=MESH)
-        return go
+        return tell
 
     others(greet(seg))
 
@@ -77,40 +105,34 @@
 
     lane = lax.broadcasted_iota(jnp.int32, (toks, LANES), 1)
     for m in range(micros):
-        xbuf[m, me, :, :width] = acts[0, m]
-        named = ids[0, m]
-        weight = gates[0, m].astype(jnp.float32)
+        named = ids[0, m].T
+        weight = gates[0, m].astype(jnp.float32).T
         spread = jnp.zeros((toks, LANES), jnp.float32)
         for k in range(named.shape[1]):
             spread = spread + jnp.where(named[:, k : k + 1] == lane, weight[:, k : k + 1], 0.0)
         xbuf[m, me, :, width:] = spread.astype(jnp.bfloat16)
 
-    @pl.when(is_last)
-    def _():
-        for m in range(micros):
-            gbuf[m, me] = out_grad[m]
-
     below, above = (seg + last) // segments, (2 * last - seg) // segments
     pl.semaphore_wait(barrier, group - 1 + group * below + group * above)
 
-    def x_copy(m, block, j):
+    def x_copy(p, block, j, slot):
         return pltpu.make_async_remote_copy(
-            xbuf.at[m, block], xbuf.at[m, block], xs.at[m, j], xr.at[m, block],
+            xbuf.at[p, block], xbuf.at[p, block], xs.at[p, slot], xr.at[p, block],
             device_id=at(seg, j), device_id_type=MESH)
 
-    def own_copy(m, block, j):
+    def own_copy(p, block, j, slot):
         return pltpu.make_async_remote_copy(
-            gbuf.at[m, block], gbuf.at[m, block], os.at[m, j], gr.at[m, block],
+            gbuf.at[p, block], gbuf.at[p, block], os.at[p, slot], gr.at[p, block],
             device_id=at(seg, j), device_id_type=MESH)
 
-    def down_copy(m, block, j):
+    def down_copy(p, block, j):
         return pltpu.make_async_remote_copy(
-            newg.at[m], gbuf.at[m, block], ds.at[m, j], gr.at[m, block],
+            newg.at[p], gbuf.at[p, block], ds.at[p, j], gr.at[p, block],
             device_id=at(lax.max(seg - 1, 0), j), device_id_type=MESH)
 
-    def r_copy(m, block, j):
+    def r_copy(p, block, j):
         return pltpu.make_async_remote_copy(
-            rst.at[m, j], rbuf.at[m, block], rs.at[m, j], rr.at[m, block],
+            rst.at[p, j], rbuf.at[p, block], rs.at[p, j], rr.at[p, block],
             device_id=at(seg, j), device_id_type=MESH)
 
     def z_copy(block, j):
@@ -118,12 +140,85 @@
             zst.at[j], zbuf.at[block], zs.at[j], zr.at[block],
             device_id=at(seg, j), device_id_type=MESH)
 
-    for m in range(micros):
-        others(lambda j: x_copy(m, me, j).start())
-
-        @pl.when(is_last)
+    def spread_own(copy, p):
+        def along(e):
+            j = e * n_fsdp + fsdp
+            copy(p, me, j, j).start()
+
+        def across(f):
+            j = expert * n_fsdp + f
+            copy(p, me, j, j).start()
+
+        other_experts(along)
+        other_fsdp(across)
+
+    def pass_on(copy, p):
+        def along(e):
+            block = e * n_fsdp + fsdp
+            copy(p, block, block, block).wait_recv()
+
+            def across(f):
+                copy(p, block, expert * n_fsdp + f, e * n_fsdp + f).start()
+
+            other_fsdp(across)
+
+        other_experts(along)
+
+    def take_rest(copy, p):
+        def across(f):
+            def along(e, carry):
+                block = e * n_fsdp + f
+                copy(p, block, block, block).wait_recv()
+                return carry
+            lax.fori_loop(0, n_expert, along, 0)
+        other_fsdp(across)
+
+    def spread_sent(copy, p):
+        others(lambda j: copy(p, me, j, j).wait_send())
+
+    def pieces(m):
+        return range(m * parts, (m + 1) * parts)
+
+    def send_loss(m):
+        for c in range(parts):
+            own_loss(m, c).wait()
+        for p in pieces(m):
+            spread_own(own_copy, p)
+
+    def pass_loss(m):
+        for p in pieces(m):
+            pass_on(own_copy, p)
+
+    def allow_next():
+        @pl.when(seg > 0)
         def _():
-            others(lambda j: own_copy(m, me, j).start())
+            pl.semaphore_signal(go, inc=1, device_id=at(seg - 1, me), device_id_type=MESH)
+
+    for copy in own_acts:
+        copy.wait()
+
+    @pl.when(is_last)
+    def _():
+        spread_own(x_copy, 0)
+        send_loss(0)
+        pass_on(x_copy, 0)
+        pass_loss(0)
+        for m in range(1, micros):
+            spread_own(x_copy, m)
+            send_loss(m)
+        take_rest(x_copy, 0)
+        allow_next()
+
+    @pl.when(seg < last)
+    def _():
+        pl.semaphore_wait(go, 1)
+        for m in range(micros):
+            spread_own(x_copy, m)
+        for m in range(micros):
+            pass_on(x_copy, m)
+        for m in range(micros):
+            take_rest(x_copy, m)
+        allow_next()
 
     stores = []
 
@@ -133,7 +228,6 @@
         stores.append(copy)
 
     def prepare(m):
-        others(lambda j: x_copy(m, j, j).wait_recv())
         x = xbuf[m, :, :, :width].reshape(rows, width)
         weights = xbuf[m, :, :, width:].reshape(rows, LANES).astype(jnp.float32)
         mine = lax.broadcasted_iota(jnp.int32, (rows, LANES), 1) == expert
@@ -150,46 +244,65 @@
             hid_buf[m, :, cut] = hidden
             hg[m, :, cut] = (hidden * c).astype(jnp.bfloat16)
 
+    def transpose(m):
+        cut = slice(m * rows, (m + 1) * rows)
+        xt[:, cut] = xbuf[m, :, :, :width].reshape(rows, width).T
+        hgt[:, cut] = hg[m].T
+
     def partial(m):
-        others(lambda j: own_copy(m, j, j).wait_recv())
-
-        @pl.when(seg < last)
-        def _():
-            own_copy(m, me, me).wait_recv()
-
-        g = gbuf[m].reshape(rows, width)
         z = jnp.zeros((rows, 1), jnp.float32)
-        for s, size in tiles:
-            cut = slice(s, s + size)
-            q = lax.dot_general(g, wd[cut, :], CONTRACT_COLS, preferred_element_type=jnp.float32)
-            da[m, :, cut] = (q * slope_buf[m, :, cut]).astype(jnp.bfloat16)
-            db[m, :, cut] = (q * act_buf[m, :, cut]).astype(jnp.bfloat16)
-            z = z + jnp.sum(q * hid_buf[m, :, cut], axis=1, keepdims=True)
-        for s, size in d_tiles:
-            cut = slice(s, s + size)
-            r = lax.dot_general(da[m], wg[cut, :], CONTRACT_COLS, preferred_element_type=jnp.float32)
-            r = r + lax.dot_general(db[m], wu[cut, :], CONTRACT_COLS, preferred_element_type=jnp.float32)
-            rst[m, :, :, cut] = r.astype(jnp.bfloat16).reshape(group, toks, size)
-        rbuf[m, me] = rst[m, me]
-        others(lambda j: r_copy(m, me, j).start())
+        for c, p in enumerate(pieces(m)):
+            @pl.when(is_last)
+            def _():
+                take_rest(own_copy, p)
+
+            @pl.when(seg < last)
+            def _():
+                members(lambda j: own_copy(p, j, j, j).wait_recv())
+
+            g = gbuf[p].reshape(rows, part_width)
+            columns = slice(c * part_width, (c + 1) * part_width)
+            for s, size in tiles:
+                cut = slice(s, s + size)
+                q = lax.dot_general(
+                    g, wd[cut, columns], CONTRACT_COLS, preferred_element_type=jnp.float32)
+                if c > 0:
+                    q = q + qbuf[:, cut]
+                if c < parts - 1:
+                    qbuf[:, cut] = q
+                else:
+                    da[m, :, cut] = (q * slope_buf[m, :, cut]).astype(jnp.bfloat16)
+                    db[m, :, cut] = (q * act_buf[m, :, cut]).astype(jnp.bfloat16)
+                    z = z + jnp.sum(q * hid_buf[m, :, cut], axis=1, keepdims=True)
+        for c, p in enumerate(pieces(m)):
+            for s, size in d_tiles:
+                cut = slice(c * part_width + s, c * part_width + s + size)
+                r = lax.dot_general(
+                    da[m], wg[cut, :], CONTRACT_COLS, preferred_element_type=jnp.float32)
+                r = r + lax.dot_general(
+                    db[m], wu[cut, :], CONTRACT_COLS, preferred_element_type=jnp.float32)
+                rst[p, :, :, s : s + size] = r.astype(jnp.bfloat16).reshape(group, toks, size)
+            others(lambda j: r_copy(p, me, j).start())
+            rbuf[p, me] = rst[p, me]
         zst[:, m] = jnp.broadcast_to(z, (rows, LANES)).astype(jnp.bfloat16).reshape(group, toks, LANES)
 
     def combine(m):
-        others(lambda j: r_copy(m, j, j).wait_recv())
-        total = gbuf[m, me].astype(jnp.float32)
-        for e in range(n_expert):
-            part = rbuf[m, e * n_fsdp].astype(jnp.float32)
-            for f in range(1, n_fsdp):
-                part = part + rbuf[m, e * n_fsdp + f].astype(jnp.float32)
-            total = total + part.astype(jnp.bfloat16).astype(jnp.float32)
-        fresh = total.astype(jnp.bfloat16)
-        newg[m] = fresh
-
-        @pl.when(seg > 0)
-        def _():
-            members(lambda j: down_copy(m, me, j).start())
-
-        act_out[0, m] = fresh
+        for c, p in enumerate(pieces(m)):
+            others(lambda j: r_copy(p, j, j).wait_recv())
+            total = gbuf[p, me].astype(jnp.float32)
+            for e in range(n_expert):
+                part = rbuf[p, e * n_fsdp].astype(jnp.float32)
+                for f in range(1, n_fsdp):
+                    part = part + rbuf[p, e * n_fsdp + f].astype(jnp.float32)
+                total = total + part.astype(jnp.bfloat16).astype(jnp.float32)
+            fresh = total.astype(jnp.bfloat16)
+            newg[p] = fresh
+
+            @pl.when(seg > 0)
+            def _():
+                members(lambda j: down_copy(p, me, j).start())
+
+            act_out[0, m, :, c * part_width : (c + 1) * part_width] = fresh
 
     for load in loads:
         load.wait()
@@ -199,27 +312,44 @@
     def _():
         for m in range(1, micros):
             prepare(m)
+
+    @pl.when(seg == 0)
+    def _():
+        for m in range(micros):
+            if m > 0 and segments == 1:
+                continue
+            transpose(m)
 
     for m in range(micros):
         if m > 0:
             @pl.when(is_last)
             def _():
+                pass_on(x_copy, m)
+                pass_loss(m)
+                take_rest(x_copy, m)
                 prepare(m)
         partial(m)
-    for m in range(micros):
-        combine(m)
 
     zbuf[me] = zst[me]
     others(lambda j: z_copy(me, j).start())
     for m in range(micros):
-        keep(xbuf.at[m, :, :, pl.ds(0, width)], x_out.at[m])
-        keep(gbuf.at[m], g_out.at[m])
+        for c, p in enumerate(pieces(m)):
+            keep(gbuf.at[p], g_out.at[m, :, :, pl.ds(c * part_width, part_width)])
         keep(da.at[m], da_out.at[m])
         keep(db.at[m], db_out.at[m])
-        keep(hg.at[m], hg_out.at[m])
+    for m in range(micros):
+        combine(m)
+
+    @pl.when((seg > 0) | (segments == 1))
+    def _():
+        for m in range(micros):
+            transpose(m)
+
+    keep(xt, xt_out)
+    keep(hgt, hgt_out)
     others(lambda j: z_copy(j, j).wait_recv())
     for m in range(micros):
-        named = ids[0, m]
+        named = ids[0, m].T
         total = jnp.zeros(named.shape, jnp.float32)
         for e in range(n_expert):
             part = zbuf[e * n_fsdp, m].astype(jnp.float32)
@@ -227,19 +357,20 @@
                 part = part + zbuf[e * n_fsdp + f, m].astype(jnp.float32)
             part = part.astype(jnp.bfloat16).astype(jnp.float32)
             total = total + jnp.where(named == e, part[:, : named.shape[1]], 0.0)
-        gate_out[0, m] = total
+        gate_out[0, m] = total.T
 
     for m in range(micros):
-        others(lambda j: x_copy(m, me, j).wait_send())
-        others(lambda j: r_copy(m, me, j).wait_send())
-
-        @pl.when(is_last)
-        def _():
-            others(lambda j: own_copy(m, me, j).wait_send())
-
-        @pl.when(seg > 0)
-        def _():
-            members(lambda j: down_copy(m, me, j).wait_send())
+        spread_sent(x_copy, m)
+        for p in pieces(m):
+            others(lambda j: r_copy(p, me, j).wait_send())
+
+            @pl.when(is_last)
+            def _():
+                spread_sent(own_copy, p)
+
+            @pl.when(seg > 0)
+            def _():
+                members(lambda j: down_copy(p, me, j).wait_send())
     others(lambda j: z_copy(me, j).wait_send())
     for copy in stores:
         copy.wait()
@@ -249,7 +380,7 @@
     micros, toks, width = acts.shape[1:]
     hid = w_gate.shape[3]
     rows = micros * group * toks
-    return 3 * width * hid * 2 + rows * (width * 2 * 4 + hid * (3 * 4 + 3 * 2) + LANES * 6)
+    return 3 * width * hid * 2 + rows * (width * 2 * 4 + hid * (4 * 4 + 4 * 2) + width * 2 + LANES * 6)
 
 
 def relay(acts, out_grad, ids, gates, w_gate, w_up, w_down):
@@ -261,6 +392,7 @@
     hid = w_gate.shape[3]
     fits = (
         toks % ROWS == 0
+        and group * toks % LANES == 0
         and width % LANES == 0
         and hid % LANES == 0
         and n_expert <= LANES
@@ -269,59 +401,64 @@
     if not fits:
         return local(acts, out_grad, ids, gates, w_gate, w_up, w_down)
     rows = group * toks
+    parts = PARTS if width % (PARTS * LANES) == 0 else 1
+    pieces = micros * parts
+    piece = (pieces, group, toks, width // parts)
     bf16, f32 = jnp.bfloat16, jnp.float32
     vmem = pl.BlockSpec(memory_space=pltpu.VMEM)
     far = pl.BlockSpec(memory_space=pl.ANY)
+    home = pl.BlockSpec(memory_space=pltpu.HBM)
     dma = pltpu.SemaphoreType.DMA
     scratch = [
         pltpu.VMEM((width, hid), bf16),
         pltpu.VMEM((width, hid), bf16),
         pltpu.VMEM((hid, width), bf16),
         pltpu.VMEM((micros, group, toks, width + LANES), bf16),
-        pltpu.VMEM((micros, group, toks, width), bf16),
-        pltpu.VMEM((micros, group, toks, width), bf16),
+        pltpu.VMEM(piece, bf16),
+        pltpu.VMEM(piece, bf16),
         pltpu.VMEM((group, micros, toks, LANES), bf16),
-        pltpu.VMEM((micros, group, toks, width), bf16),
+        pltpu.VMEM(piece, bf16),
         pltpu.VMEM((group, micros, toks, LANES), bf16),
-        pltpu.VMEM((micros, toks, width), bf16),
+        pltpu.VMEM((pieces, toks, width // parts), bf16),
     ]
     scratch += [pltpu.VMEM((micros, rows, hid), f32)] * 3
+    scratch += [pltpu.VMEM((rows, hid), f32)]
     scratch += [pltpu.VMEM((micros, rows, hid), bf16)] * 3
-    scratch += [dma((3,)), dma((5 * micros,))]
-    scratch += [dma((micros, group))] * 7
+    scratch += [pltpu.VMEM((width, micros * rows), bf16), pltpu.VMEM((hid, micros * rows), bf16)]
+    scratch += [dma((3 + micros + pieces,)), dma((2 + 2 * micros + pieces,))]
+    scratch += [pltpu.SemaphoreType.REGULAR]
+    scratch += [dma((micros, group))] * 2
+    scratch += [dma((pieces, group))] * 5
     scratch += [dma((group,))] * 2
     flops = 2 * micros * rows * width * hid * 5
     outs = pl.pallas_call(
         functools.partial(relay_kernel, segments, n_expert, n_fsdp),
         out_shape=(
             jax.ShapeDtypeStruct(acts.shape, bf16),
-            jax.ShapeDtypeStruct(gates.shape, f32),
-            jax.ShapeDtypeStruct((micros, group, toks, width), bf16),
+            jax.ShapeDtypeStruct(gates.shape[:2] + (gates.shape[3], toks), f32),
+            jax.ShapeDtypeStruct((width, micros * rows), bf16),
             jax.ShapeDtypeStruct((micros, group, toks, width), bf16),
             jax.ShapeDtypeStruct((micros, rows, hid), bf16),
             jax.ShapeDtypeStruct((micros, rows, hid), bf16),
-            jax.ShapeDtypeStruct((micros, rows, hid), bf16),
+            jax.ShapeDtypeStruct((hid, micros * rows), bf16),
         ),
-        in_specs=[vmem, vmem, vmem, vmem, far, far, far],
+        in_specs=[home, home, vmem, vmem, far, far, far],
         out_specs=(vmem, vmem, far, far, far, far, far),
         scratch_shapes=scratch,
         compiler_params=pltpu.CompilerParams(
-            collective_id=0, has_side_effects=True, vmem_limit_bytes=ROOM + (8 << 20)
+            collective_id=0, has_side_effects=True, vmem_limit_bytes=GRANT
         ),
         cost_estimate=pl.CostEstimate(
             flops=flops, bytes_accessed=6 * width * hid, transcendentals=micros * rows * hid
         ),
-    )(acts, out_grad, ids, gates, w_gate, w_up, w_down)
-    act_grad, gate_grad, x, g, da, db, hg = outs
-    x = x.reshape(-1, width)
-    g = g.reshape(-1, width)
+    )(acts, out_grad, ids.swapaxes(2, 3), gates.swapaxes(2, 3), w_gate, w_up, w_down)
+    act_grad, gate_grad, xt, g, da, db, hgt = outs
 
     def weight_grad(left, right):
-        total = lax.dot_general(left, right, CONTRACT_ROWS, preferred_element_type=f32)
+        total = jnp.dot(left, right.reshape(micros * rows, -1), preferred_element_type=f32)
         return total.astype(bf16)[None, None]
 
-    da, db, hg = (v.reshape(-1, hid) for v in (da, db, hg))
-    return act_grad, gate_grad, weight_grad(x, da), weight_grad(x, db), weight_grad(hg, g)
+    return act_grad, gate_grad.swapaxes(2, 3), weight_grad(xt, da), weight_grad(xt, db), weight_grad(hgt, g)
 
 
 def from_behind(value, axis, steps):

time: 94.7 us -> 87.8 us (0.927)
  Pallas kernels: 82 us -> 78.4 us
  local copies, waits for them, and re-layouts: 4.51 us -> 1.23 us
    pallas_call x1, Pallas kernels: 82 us -> 78.4 us  [relay(): pl.pallas_call(functools.partial(relay_kernel, segments, n_expert, n_fsdp...]
    unnamed x10 -> x14, local copies, waits for them, and re-layouts: 4.51 us -> 1.23 us
where the time goes in v2:
time: 87.8 us; the launch traced here: 87.7 us
  Pallas kernels  78.4 us (89%)
  matrix products  7.38 us (8%)
  local copies, waits for them, and re-layouts  1.23 us (1%)
    pallas_call x1, Pallas kernels, relay(): pl.pallas_call(functools.partial(relay_kernel, segments, n_expert, n_fsdp...  78.4 us
    dot_general x3, matrix products, weight_grad(): jnp.dot(left, right.reshape(micros * rows, -1), preferred_element_type=f32)  7.38 us

profile of v2, /device:TPU:0, one launch (start us, length us, event | category | flops | bytes accessed | tf_op | source)
XLA Modules:
  0.0 87.7 jit_solution(473853041298507275)
XLA Ops:
  0.6 78.4 %shard_map.110 = (bf16[1,2,16,1024]{3,2,1,0:T(8,128)(2,1)}, f32[1,2,2,16]{3,2,1,0:T(2,128)}, bf16[1024,256]{1,0:T(8,128)(2,1)}, bf16[2,8,16,1024]{3,2,1,0:T(8,12...) custom-call(bf16[1,2,16,1024]{3,2,1,0:T(8,128)(2,1)} %acts.1, ...), custom_call_target="tpu_custom_call" | custom-call | flops 2684354560 | bytes 6291456 | tf_op jit(solution)/shard_map/pallas_call | solution.py:434
  79.0 0.0 copy-start
  79.0 0.0 copy-start.3
  79.0 3.3 %convert_bitcast_fusion.2 = bf16[1,1,1024,1024]{3,2,1,0:T(8,128)(2,1)} fusion(bf16[1024,256]{1,0:T(8,128)(2,1)} %get-tuple-element.14, bf16[256,1024]{1,0:T(8,128)(2,1)} %bitcast.20), kind=kOutput, calls=%fused_computation.2 | convolution fusion | flops 537919488 | bytes 3145728 | tf_op jit(solution)/shard_map/dot_general | solution.py:458
  82.3 0.0 copy-done
  82.3 0.0 copy-done.3
  82.4 0.0 copy-start.1
  82.4 0.0 copy-start.2
  82.4 2.0 %convert_bitcast_fusion.1 = bf16[1,1,1024,1024]{3,2,1,0:T(8,128)(2,1)} fusion(bf16[1024,256]{1,0:T(8,128)(2,1)S(1)} %copy-done, bf16[256,1024]{1,0:T(8,128)(2,1)S(1)} %bitcast.19), kind=kOutput, calls=%fused_computation.1 | convolution fusion | flops 537919488 | bytes 3145728 | tf_op jit(solution)/shard_map/dot_general | solution.py:458
  84.4 0.0 copy-done.1
  84.4 0.0 copy-done.2
  84.4 0.0 copy-start.4
  84.4 0.0 copy-start.5
  84.4 2.0 %convert_bitcast_fusion = bf16[1,1,1024,1024]{3,2,1,0:T(8,128)(2,1)} fusion(bf16[1024,256]{1,0:T(8,128)(2,1)S(1)} %copy-done.2, bf16[256,1024]{1,0:T(8,128)(2,1)S(1)} %bitcast.18), kind=kOutput, calls=%fused_computation | convolution fusion | flops 537919488 | bytes 3145728 | tf_op jit(solution)/shard_map/dot_general | solution.py:458
  86.4 0.0 copy-done.4
  86.4 0.6 copy.14
  87.1 0.0 copy-done.5
  87.1 0.6 copy.15
Async XLA Ops:
  79.0 3.3 %copy-start = (bf16[1024,256]{1,0:T(8,128)(2,1)S(1)}, bf16[1024,256]{1,0:T(8,128)(2,1)}, u32[]{:S(2)}) copy-start(bf16[1024,256]{1,0:T(8,128)(2,1)} %get-tuple-element.14) | copy-start | bytes 1572868
  79.0 3.3 %copy-start.3 = (bf16[2,128,1024]{2,1,0:T(8,128)(2,1)S(1)}, bf16[2,128,1024]{2,1,0:T(8,128)(2,1)}, u32[]{:S(2)}) copy-start(bf16[2,128,1024]{2,1,0:T(8,128)(2,1)} %get-tuple-element.16) | copy-start | bytes 1572868
  82.4 2.0 %copy-start.1 = (bf16[2,8,16,1024]{3,2,1,0:T(8,128)(2,1)S(1)}, bf16[2,8,16,1024]{3,2,1,0:T(8,128)(2,1)}, u32[]{:S(2)}) copy-start(bf16[2,8,16,1024]{3,2,1,0:T(8,128)(2,1)} %get-tuple-element.18) | copy-start | bytes 1572868
  82.4 2.0 %copy-start.2 = (bf16[1024,256]{1,0:T(8,128)(2,1)S(1)}, bf16[1024,256]{1,0:T(8,128)(2,1)}, u32[]{:S(2)}) copy-start(bf16[1024,256]{1,0:T(8,128)(2,1)} %get-tuple-element.17) | copy-start | bytes 1572868
  84.4 2.0 %copy-start.4 = (bf16[1,2,16,1024]{3,2,1,0:T(8,128)(2,1)S(1)}, bf16[1,2,16,1024]{3,2,1,0:T(8,128)(2,1)}, u32[]{:S(2)}) copy-start(bf16[1,2,16,1024]{3,2,1,0:T(8,128)(2,1)} %get-tuple-element.24) | copy-start | bytes 196612
  84.4 2.7 %copy-start.5 = (f32[1,2,2,16]{3,2,1,0:T(2,128)S(1)}, f32[1,2,2,16]{3,2,1,0:T(2,128)}, u32[]{:S(2)}) copy-start(f32[1,2,2,16]{3,2,1,0:T(2,128)} %get-tuple-element.13) | copy-start | bytes 772

commit v3 on v2

--- a/solution.py
+++ b/solution.py
@@ -199,13 +199,11 @@
 
     @pl.when(is_last)
     def _():
-        spread_own(x_copy, 0)
-        send_loss(0)
+        for m in range(micros):
+            spread_own(x_copy, m)
+            send_loss(m)
         pass_on(x_copy, 0)
         pass_loss(0)
-        for m in range(1, micros):
-            spread_own(x_copy, m)
-            send_loss(m)
         take_rest(x_copy, 0)
         allow_next()
 
@@ -308,6 +306,12 @@
         load.wait()
     prepare(0)
 
+    @pl.when(is_last)
+    def _():
+        for m in range(1, micros):
+            pass_on(x_copy, m)
+            pass_loss(m)
+
     @pl.when(seg < last)
     def _():
         for m in range(1, micros):
@@ -316,16 +320,13 @@
     @pl.when(seg == 0)
     def _():
         for m in range(micros):
-            if m > 0 and segments == 1:
-                continue
-            transpose(m)
+            if segments > 1:
+                transpose(m)
 
     for m in range(micros):
         if m > 0:
             @pl.when(is_last)
             def _():
-                pass_on(x_copy, m)
-                pass_loss(m)
                 take_rest(x_copy, m)
                 prepare(m)
         partial(m)
@@ -337,16 +338,28 @@
             keep(gbuf.at[p], g_out.at[m, :, :, pl.ds(c * part_width, part_width)])
         keep(da.at[m], da_out.at[m])
         keep(db.at[m], db_out.at[m])
+    turned = [
+        pltpu.make_async_copy(src, dst, out_sem.at[len(stores) + i])
+        for i, (src, dst) in enumerate(((xt, xt_out), (hgt, hgt_out)))
+    ]
+    early = seg + (segments == 1) == 0
+    late = seg + (segments == 1) > 0
+
+    @pl.when(early)
+    def _():
+        for copy in turned:
+            copy.start()
+
     for m in range(micros):
         combine(m)
 
-    @pl.when((seg > 0) | (segments == 1))
+    @pl.when(late)
     def _():
         for m in range(micros):
             transpose(m)
-
-    keep(xt, xt_out)
-    keep(hgt, hgt_out)
+        for copy in turned:
+            copy.start()
+
     others(lambda j: z_copy(j, j).wait_recv())
     for m in range(micros):
         named = ids[0, m].T
@@ -372,8 +385,82 @@
             def _():
                 members(lambda j: down_copy(p, me, j).wait_send())
     others(lambda j: z_copy(me, j).wait_send())
+    for copy in stores + turned:
+        copy.wait()
+
+
+def weight_kernel(
+    xt, da, db, hgt, g, act, gate, grad_gate, grad_up, grad_down, act_out, gate_out,
+    xt_v, da_v, db_v, hgt_v, g_v, made, in_sem, out_sem,
+):
+    loads = [
+        pltpu.make_async_copy(src, dst, in_sem.at[i])
+        for i, (src, dst) in enumerate(((xt, xt_v), (da, da_v), (db, db_v), (hgt, hgt_v), (g, g_v)))
+    ]
+    for load in loads:
+        load.start()
+    stores = [
+        pltpu.make_async_copy(src, dst, out_sem.at[i])
+        for i, (src, dst) in enumerate(((act, act_out), (gate, gate_out)))
+    ]
+    for copy in stores:
+        copy.start()
+    products = (
+        (xt_v, da_v, grad_gate, loads[:2]),
+        (xt_v, db_v, grad_up, loads[2:3]),
+        (hgt_v, g_v, grad_down, loads[3:]),
+    )
+    base = 0
+    for left, right, result, needed in products:
+        for load in needed:
+            load.wait()
+        height, columns = left.shape[0], right.shape[1]
+        for s in range(0, height, TILE):
+            size = min(TILE, height - s)
+            tile = jnp.dot(left[s : s + size, :], right[...], preferred_element_type=jnp.float32)
+            place = made.at[pl.ds(base + s, size), pl.ds(0, columns)]
+            place[...] = tile.astype(jnp.bfloat16)
+            copy = pltpu.make_async_copy(
+                place, result.at[0, 0, pl.ds(s, size)], out_sem.at[len(stores)])
+            copy.start()
+            stores.append(copy)
+        base += height
     for copy in stores:
         copy.wait()
+
+
+def weight_grads(xt, da, db, hgt, g, act, gate):
+    width, rows = xt.shape
+    hid = da.shape[1]
+    bf16 = jnp.bfloat16
+    far = pl.BlockSpec(memory_space=pl.ANY)
+    stores = 2 + 2 * -(-width // TILE) + -(-hid // TILE)
+    return pl.pallas_call(
+        weight_kernel,
+        out_shape=(
+            jax.ShapeDtypeStruct((1, 1, width, hid), bf16),
+            jax.ShapeDtypeStruct((1, 1, width, hid), bf16),
+            jax.ShapeDtypeStruct((1, 1, hid, width), bf16),
+            jax.ShapeDtypeStruct(act.shape, act.dtype),
+            jax.ShapeDtypeStruct(gate.shape, gate.dtype),
+        ),
+        in_specs=[far] * 7,
+        out_specs=(far,) * 5,
+        scratch_shapes=[
+            pltpu.VMEM((width, rows), bf16),
+            pltpu.VMEM((rows, hid), bf16),
+            pltpu.VMEM((rows, hid), bf16),
+            pltpu.VMEM((hid, rows), bf16),
+            pltpu.VMEM((rows, width), bf16),
+            pltpu.VMEM((2 * width + hid, max(width, hid)), bf16),
+            pltpu.SemaphoreType.DMA((5,)),
+            pltpu.SemaphoreType.DMA((stores,)),
+        ],
+        compiler_params=pltpu.CompilerParams(vmem_limit_bytes=GRANT),
+        cost_estimate=pl.CostEstimate(
+            flops=6 * rows * width * hid, bytes_accessed=6 * width * hid, transcendentals=0
+        ),
+    )(xt, da, db, hgt, g, act, gate)
 
 
 def relay_room(acts, w_gate, group):
@@ -454,11 +541,9 @@
     )(acts, out_grad, ids.swapaxes(2, 3), gates.swapaxes(2, 3), w_gate, w_up, w_down)
     act_grad, gate_grad, xt, g, da, db, hgt = outs
 
-    def weight_grad(left, right):
-        total = jnp.dot(left, right.reshape(micros * rows, -1), preferred_element_type=f32)
-        return total.astype(bf16)[None, None]
-
-    return act_grad, gate_grad.swapaxes(2, 3), weight_grad(xt, da), weight_grad(xt, db), weight_grad(hgt, g)
+    grad_gate, grad_up, grad_down, act_grad, gate_grad = weight_grads(
+        xt, da.reshape(-1, hid), db.reshape(-1, hid), hgt, g.reshape(-1, width), act_grad, gate_grad)
+    return act_grad, gate_grad.swapaxes(2, 3), grad_gate, grad_up, grad_down
 
 
 def from_behind(value, axis, steps):

time: 87.8 us -> 80.7 us (0.919)
  matrix products: 7.38 us -> 0 us
  Pallas kernels: 78.4 us -> 79.8 us
  local copies, waits for them, and re-layouts: 1.23 us -> 0 us
    dot_general x3 -> x0, matrix products: 7.38 us -> none  [weight_grad(): jnp.dot(left, right.reshape(micros * rows, -1), preferred_element_type=f32)]
    pallas_call x0 -> x1, Pallas kernels: none -> 4.37 us  [weight_grads(): pl.pallas_call(weight_kernel, out_shape=(jax.ShapeDtypeStruct((1, 1, widt...]
    pallas_call x1, Pallas kernels: 78.4 us -> 75.5 us  [relay(): pl.pallas_call(functools.partial(relay_kernel, segments, n_expert, n_fsdp...]
    unnamed x14 -> x0, local copies, waits for them, and re-layouts: 1.23 us -> none
where the time goes in v3:
time: 80.7 us; the launch traced here: 80.5 us
  Pallas kernels  79.8 us (99%)
    pallas_call x1, Pallas kernels, relay(): pl.pallas_call(functools.partial(relay_kernel, segments, n_expert, n_fsdp...  75.5 us
    pallas_call x1, Pallas kernels, weight_grads(): pl.pallas_call(weight_kernel, out_shape=(jax.ShapeDtypeStruct((1, 1, widt...  4.37 us

profile of v3, /device:TPU:0, one launch (start us, length us, event | category | flops | bytes accessed | tf_op | source)
XLA Modules:
  0.0 80.5 jit_solution(11698359154641410761)
XLA Ops:
  0.6 75.5 %shard_map.110 = (bf16[1,2,16,1024]{3,2,1,0:T(8,128)(2,1)}, f32[1,2,2,16]{3,2,1,0:T(2,128)}, bf16[1024,256]{1,0:T(8,128)(2,1)}, bf16[2,8,16,1024]{3,2,1,0:T(8,12...) custom-call(bf16[1,2,16,1024]{3,2,1,0:T(8,128)(2,1)} %acts.1, ...), custom_call_target="tpu_custom_call" | custom-call | flops 2684354560 | bytes 6291456 | tf_op jit(solution)/shard_map/pallas_call | solution.py:521
  76.1 4.4 %shard_map.111 = (bf16[1,1,1024,1024]{3,2,1,0:T(8,128)(2,1)}, bf16[1,1,1024,1024]{3,2,1,0:T(8,128)(2,1)}, bf16[1,1,1024,1024]{3,2,1,0:T(8,128)(2,1)}, bf16[1,2,16,1024]{3,2,1,0:T(8,128)(2,1)}, f32[1,2,2,16]{3,2,1,0:T(2,128)}) custom-call(bf16[1024,256]{1,0:T(8,128)(2,1)} %get-tuple-element.17.xt, bf16[256,1024]{1,0:T(8,128)(2,1)} %bitcast.9, ...), custom_call_target="tpu_custom_call" | custom-call | flops 1610612736 | bytes 6291456 | tf_op jit(solution)/shard_map/pallas_call | solution.py:438

commit v4 on v3

--- a/solution.py
+++ b/solution.py
@@ -22,7 +22,7 @@
     acts, out_grad, ids, gates, w_gate, w_up, w_down,
     act_out, gate_out, xt_out, g_out, da_out, db_out, hgt_out,
     wg, wu, wd, xbuf, gbuf, rbuf, zbuf, rst, zst, newg,
-    slope_buf, act_buf, hid_buf, qbuf, da, db, hg, xt, hgt,
+    slope_buf, act_buf, hid_buf, qbuf, da, db, hg, xt, hgt, wgt, wut, wdt,
     in_sem, out_sem, go, xs, xr, os, gr, ds, rs, rr, zs, zr,
 ):
     group = n_expert * n_fsdp
@@ -207,8 +207,15 @@
         take_rest(x_copy, 0)
         allow_next()
 
+    for load in loads:
+        load.wait()
+
     @pl.when(seg < last)
     def _():
+        for src, dst in ((wg, wgt), (wu, wut), (wd, wdt)):
+            for s in range(0, src.shape[0], TILE):
+                e = min(s + TILE, src.shape[0])
+                dst[:, s:e] = src[s:e, :].T
         pl.semaphore_wait(go, 1)
         for m in range(micros):
             spread_own(x_copy, m)
@@ -247,23 +254,25 @@
         xt[:, cut] = xbuf[m, :, :, :width].reshape(rows, width).T
         hgt[:, cut] = hg[m].T
 
-    def partial(m):
+    def times(left, kept, turned, cut, along, flat):
+        if flat:
+            return lax.dot_general(
+                left, kept[cut, along], CONTRACT_COLS, preferred_element_type=jnp.float32)
+        return jnp.dot(left, turned[along, cut], preferred_element_type=jnp.float32)
+
+    def partial(m, flat):
         z = jnp.zeros((rows, 1), jnp.float32)
         for c, p in enumerate(pieces(m)):
-            @pl.when(is_last)
-            def _():
+            if flat:
                 take_rest(own_copy, p)
-
-            @pl.when(seg < last)
-            def _():
+            else:
                 members(lambda j: own_copy(p, j, j, j).wait_recv())
 
             g = gbuf[p].reshape(rows, part_width)
             columns = slice(c * part_width, (c + 1) * part_width)
             for s, size in tiles:
                 cut = slice(s, s + size)
-                q = lax.dot_general(
-                    g, wd[cut, columns], CONTRACT_COLS, preferred_element_type=jnp.float32)
+                q = times(g, wd, wdt, cut, columns, flat)
                 if c > 0:
                     q = q + qbuf[:, cut]
                 if c < parts - 1:
@@ -275,10 +284,8 @@
         for c, p in enumerate(pieces(m)):
             for s, size in d_tiles:
                 cut = slice(c * part_width + s, c * part_width + s + size)
-                r = lax.dot_general(
-                    da[m], wg[cut, :], CONTRACT_COLS, preferred_element_type=jnp.float32)
-                r = r + lax.dot_general(
-                    db[m], wu[cut, :], CONTRACT_COLS, preferred_element_type=jnp.float32)
+                r = times(da[m], wg, wgt, cut, slice(None), flat)
+                r = r + times(db[m], wu, wut, cut, slice(None), flat)
                 rst[p, :, :, s : s + size] = r.astype(jnp.bfloat16).reshape(group, toks, size)
             others(lambda j: r_copy(p, me, j).start())
             rbuf[p, me] = rst[p, me]
@@ -302,8 +309,6 @@
 
             act_out[0, m, :, c * part_width : (c + 1) * part_width] = fresh
 
-    for load in loads:
-        load.wait()
     prepare(0)
 
     @pl.when(is_last)
@@ -329,7 +334,15 @@
             def _():
                 take_rest(x_copy, m)
                 prepare(m)
-        partial(m)
+
+        @pl.when(is_last)
+        def _():
+            partial(m, True)
+
+        if segments > 1:
+            @pl.when(seg < last)
+            def _():
+                partial(m, False)
 
     zbuf[me] = zst[me]
     others(lambda j: z_copy(me, j).start())
@@ -467,7 +480,7 @@
     micros, toks, width = acts.shape[1:]
     hid = w_gate.shape[3]
     rows = micros * group * toks
-    return 3 * width * hid * 2 + rows * (width * 2 * 4 + hid * (4 * 4 + 4 * 2) + width * 2 + LANES * 6)
+    return 6 * width * hid * 2 + rows * (width * 2 * 4 + hid * (4 * 4 + 4 * 2) + width * 2 + LANES * 6)
 
 
 def relay(acts, out_grad, ids, gates, w_gate, w_up, w_down):
@@ -512,6 +525,7 @@
     scratch += [pltpu.VMEM((rows, hid), f32)]
     scratch += [pltpu.VMEM((micros, rows, hid), bf16)] * 3
     scratch += [pltpu.VMEM((width, micros * rows), bf16), pltpu.VMEM((hid, micros * rows), bf16)]
+    scratch += [pltpu.VMEM((hid, width), bf16)] * 2 + [pltpu.VMEM((width, hid), bf16)]
     scratch += [dma((3 + micros + pieces,)), dma((2 + 2 * micros + pieces,))]
     scratch += [pltpu.SemaphoreType.REGULAR]
     scratch += [dma((micros, group))] * 2

time: 80.7 us -> 79.3 us (0.983)
  Pallas kernels: 79.8 us -> 78.4 us
    pallas_call x1, Pallas kernels: 75.5 us -> 74 us  [relay(): pl.pallas_call(functools.partial(relay_kernel, segments, n_expert, n_fsdp...]
where the time goes in v4:
time: 79.3 us; the launch traced here: 79.2 us
  Pallas kernels  78.4 us (99%)
  between operations  0.8 us (1%)
    pallas_call x1, Pallas kernels, relay(): pl.pallas_call(functools.partial(relay_kernel, segments, n_expert, n_fsdp...  74 us
    pallas_call x1, Pallas kernels, weight_grads(): pl.pallas_call(weight_kernel, out_shape=(jax.ShapeDtypeStruct((1, 1, widt...  4.37 us

profile of v4, /device:TPU:0, one launch (start us, length us, event | category | flops | bytes accessed | tf_op | source)
XLA Modules:
  0.0 79.2 jit_solution(16301486689432021654)
XLA Ops:
  0.6 74.0 %shard_map.110 = (bf16[1,2,16,1024]{3,2,1,0:T(8,128)(2,1)}, f32[1,2,2,16]{3,2,1,0:T(2,128)}, bf16[1024,256]{1,0:T(8,128)(2,1)}, bf16[2,8,16,1024]{3,2,1,0:T(8,12...) custom-call(bf16[1,2,16,1024]{3,2,1,0:T(8,128)(2,1)} %acts.1, ...), custom_call_target="tpu_custom_call" | custom-call | flops 2684354560 | bytes 6291456 | tf_op jit(solution)/shard_map/pallas_call | solution.py:535
  74.6 4.4 %shard_map.111 = (bf16[1,1,1024,1024]{3,2,1,0:T(8,128)(2,1)}, bf16[1,1,1024,1024]{3,2,1,0:T(8,128)(2,1)}, bf16[1,1,1024,1024]{3,2,1,0:T(8,128)(2,1)}, bf16[1,2,16,1024]{3,2,1,0:T(8,128)(2,1)}, f32[1,2,2,16]{3,2,1,0:T(2,128)}) custom-call(bf16[1024,256]{1,0:T(8,128)(2,1)} %get-tuple-element.17.xt, bf16[256,1024]{1,0:T(8,128)(2,1)} %bitcast.9, ...), custom_call_target="tpu_custom_call" | custom-call | flops 1610612736 | bytes 6291456 | tf_op jit(solution)/shard_map/pallas_call | solution.py:451

commit v5 on v4

--- a/solution.py
+++ b/solution.py
@@ -13,7 +13,7 @@
 TILE = 256
 GRANT = 62 << 20
 ROOM = 44 << 20
-PARTS = 2
+PARTS = 1
 CONTRACT_COLS = (((1,), (1,)), ((), ()))
 
 

time: 79.3 us -> 76.2 us (0.961)
  Pallas kernels: 78.4 us -> 75.4 us
    pallas_call x1, Pallas kernels: 74 us -> 71 us  [relay(): pl.pallas_call(functools.partial(relay_kernel, segments, n_expert, n_fsdp...]
where the time goes in v5:
time: 76.2 us; the launch traced here: 76 us
  Pallas kernels  75.4 us (99%)
    pallas_call x1, Pallas kernels, relay(): pl.pallas_call(functools.partial(relay_kernel, segments, n_expert, n_fsdp...  71 us
    pallas_call x1, Pallas kernels, weight_grads(): pl.pallas_call(weight_kernel, out_shape=(jax.ShapeDtypeStruct((1, 1, widt...  4.37 us

profile of v5, /device:TPU:0, one launch (start us, length us, event | category | flops | bytes accessed | tf_op | source)
XLA Modules:
  0.0 76.0 jit_solution(17136985739192899789)
XLA Ops:
  0.6 71.0 %shard_map.110 = (bf16[1,2,16,1024]{3,2,1,0:T(8,128)(2,1)}, f32[1,2,2,16]{3,2,1,0:T(2,128)}, bf16[1024,256]{1,0:T(8,128)(2,1)}, bf16[2,8,16,1024]{3,2,1,0:T(8,12...) custom-call(bf16[1,2,16,1024]{3,2,1,0:T(8,128)(2,1)} %acts.1, ...), custom_call_target="tpu_custom_call" | custom-call | flops 2684354560 | bytes 6291456 | tf_op jit(solution)/shard_map/pallas_call | solution.py:535
  71.7 4.4 %shard_map.111 = (bf16[1,1,1024,1024]{3,2,1,0:T(8,128)(2,1)}, bf16[1,1,1024,1024]{3,2,1,0:T(8,128)(2,1)}, bf16[1,1,1024,1024]{3,2,1,0:T(8,128)(2,1)}, bf16[1,2,16,1024]{3,2,1,0:T(8,128)(2,1)}, f32[1,2,2,16]{3,2,1,0:T(2,128)}) custom-call(bf16[1024,256]{1,0:T(8,128)(2,1)} %get-tuple-element.17.xt, bf16[256,1024]{1,0:T(8,128)(2,1)} %bitcast.9, ...), custom_call_target="tpu_custom_call" | custom-call | flops 1610612736 | bytes 6291456 | tf_op jit(solution)/shard_map/pallas_call | solution.py:451
